TPU v7x, 256 devices: a whole 4x4x8 slice. The times are simulated.
256 devices in a mesh: replica: 16 (over x_hi, y, core), tensor: 16 (over z, x_lo).
Axes of the slice: x: 4 (x_hi: 2, x_lo: 2; x = x_hi * 2 + x_lo), y: 4, z: 8, core: 2. Of those that a mesh axis runs over, the one named last changes fastest.
Arguments:
- hidden: bfloat16 [2, 16, 4, 8192], P(None, 'replica', None, 'tensor'), may hold values from -12 to 12
- resident: bfloat16 [2, 8192, 2048], P(None, 'tensor'), may hold values from -6 to 6
- delta_codes: bfloat16 [2, 8192, 2048], P(None, 'tensor', 'replica'), may hold values from -4 to 4
- scales: bfloat16 [2, 8192, 16], P(None, 'tensor', 'replica'), may hold values from 0.049804688 to 0.5
- owner_map: int32 [16], replicated, may hold values from 0 to 15, each once
- key_value_bias: bfloat16 [2, 2048], replicated, may hold values from -6 to 6
- queries: bfloat16 [2, 16, 4, 64, 128], P(None, 'replica'), may hold values from -110 to 110
- key_cache: bfloat16 [2, 16, 8192, 8, 128], P(None, 'replica', 'tensor'), may hold values from -5 to 5
- value_cache: bfloat16 [2, 16, 8192, 8, 128], P(None, 'replica', 'tensor'), may hold values from -5 to 5
- lengths: int32 [16], P('replica'), may hold values from 1024 to 8188, as said below
Outputs:
- updated_weights: bfloat16 [2, 8192, 2048], P(None, 'tensor')
- attention_out: bfloat16 [2, 16, 4, 64, 128], P(None, 'replica', None, 'tensor')
Inputs may be any that keep to these rules, and one draw needn't show every extreme that they name: owner_map is a permutation of 0 to 15. `lengths`: sequence 0 has exactly 8188 filled slots.
All inputs are finite; a program needn't handle non-finite values.
Results may differ from a plain program's by a relative error of at most 0.008.
Values may be sent and summed in bfloat16 or wider, within the bound.
A program may use at most 128 MiB of HBM per device.

v0:
```python
import jax
import jax.numpy as jnp
from jax import lax
from jax.sharding import PartitionSpec as P

D = 8192


ROPE_BASE = 1000000.0


def combined_all(part, axis, combine):
    gathered = jax.tree.map(lambda a: lax.all_gather(a, axis), part)

    def take(source):
        return jax.tree.map(lambda a: lax.dynamic_index_in_dim(a, source, 0, False), gathered)

    return lax.fori_loop(
        1, lax.axis_size(axis), lambda source, state: combine(state, take(source)), take(0)
    )


def rotate(values, positions, is_key):
    half = values.shape[-1] // 2
    index_range = jnp.arange(half).astype(jnp.float32)
    inverse = ROPE_BASE ** (-2.0 * index_range / values.shape[-1])
    angle = positions[:, None] * inverse[None, :]
    cosine = jnp.cos(angle)[:, None, :]
    sine = jnp.sin(angle)[:, None, :]
    former = values[..., :half]
    latter = values[..., half:]
    turned = jnp.concatenate(
        [former * cosine - latter * sine, latter * cosine + former * sine], axis=-1
    )
    return jnp.where(is_key[None, :, None], turned, values)


def apply_delta(layer_codes, layer_scales, resident_rows, owner_map, replicas, head_size):
    local_rows, width = resident_rows.shape
    group_cols = width // replicas
    group_blocks = layer_scales.shape[1] // replicas
    slot_codes = jnp.take(layer_codes.reshape(local_rows, replicas, group_cols), owner_map, axis=1)
    slot_scales = jnp.take(
        layer_scales.reshape(local_rows, replicas, group_blocks), owner_map, axis=1
    )
    delta_full = slot_codes.astype(jnp.float32)
    delta_full = (
        delta_full
        * slot_scales.reshape(local_rows, width // head_size).astype(jnp.float32)[:, :, None]
    )
    return (resident_rows.astype(jnp.float32) + delta_full.reshape(local_rows, width)).astype(
        jnp.bfloat16
    )


def joined(former, latter):
    high_a, total_a, summed_a = former
    high_b, total_b, summed_b = latter
    highest = jnp.maximum(high_a, high_b)
    factor_a = jnp.exp(high_a - highest)
    factor_b = jnp.exp(high_b - highest)
    return (
        highest,
        total_a * factor_a + total_b * factor_b,
        summed_a * factor_a[..., None] + summed_b * factor_b[..., None],
    )


def partial_attention(
    query, cached_keys, cached_values, new_keys, new_values, local_lengths, tensor_index
):
    seq_dev, steps, heads, head_size = query.shape
    kv_heads = cached_keys.shape[2]
    cache_local = cached_keys.shape[1]
    score_scale = head_size ** (-0.5)
    grouped = query.reshape(seq_dev, steps, kv_heads, heads // kv_heads, head_size)
    scores = (
        jnp.einsum("bsghd,bpgd->bsghp", grouped, cached_keys, preferred_element_type=jnp.float32)
        * score_scale
    )
    cache_spots = tensor_index * cache_local + jnp.arange(cache_local)
    inside = cache_spots[None, :] < local_lengths[:, None]
    scores = jnp.where(inside[:, None, None, None, :], scores, -1e30)
    fresh_scores = (
        jnp.einsum("bsghd,bjgd->bsghj", grouped, new_keys, preferred_element_type=jnp.float32)
        * score_scale
    )
    allowed = (jnp.arange(steps)[None, :] <= jnp.arange(steps)[:, None]) & (tensor_index == 0)
    fresh_scores = jnp.where(allowed[None, :, None, None, :], fresh_scores, -1e30)
    highest = jnp.maximum(jnp.max(scores, axis=-1), jnp.max(fresh_scores, axis=-1))
    expo = jnp.exp(scores - highest[..., None])
    fresh_expo = jnp.exp(fresh_scores - highest[..., None])
    denominator = jnp.sum(expo, axis=-1) + jnp.sum(fresh_expo, axis=-1)
    summed = jnp.einsum(
        "bsghp,bpgd->bsghd",
        expo.astype(jnp.bfloat16),
        cached_values,
        preferred_element_type=jnp.float32,
    )
    summed = summed + jnp.einsum(
        "bsghj,bjgd->bsghd",
        fresh_expo.astype(jnp.bfloat16),
        new_values,
        preferred_element_type=jnp.float32,
    )
    return (
        highest.reshape(seq_dev, steps, heads),
        denominator.reshape(seq_dev, steps, heads),
        summed.reshape(seq_dev, steps, heads, head_size),
    )


def on_device(
    hidden,
    resident,
    delta_codes,
    scales,
    owner_map,
    key_value_bias,
    queries,
    key_cache,
    value_cache,
    lengths,
):
    replicas = lax.axis_size("replica")
    tensor_count = lax.axis_size("tensor")
    tensor_index = lax.axis_index("tensor")
    layer_count, local_rows, width = resident.shape
    seq_dev, steps = (hidden.shape[1], hidden.shape[2])
    heads, head_size = (queries.shape[3], queries.shape[4])
    pair_count = width // head_size
    kv_heads = pair_count // 2
    own_heads = heads // tensor_count
    width_scale = D ** (-0.5)
    positions = (lengths[:, None] + jnp.arange(steps)[None, :]).reshape(-1).astype(jnp.float32)
    weight_list = []
    output_list = []
    for layer_index in range(layer_count):
        layer_codes, layer_scales = (
            lax.all_gather(delta_codes[layer_index], "replica", axis=1, tiled=True),
            lax.all_gather(scales[layer_index], "replica", axis=1, tiled=True),
        )
        refreshed = apply_delta(
            layer_codes, layer_scales, resident[layer_index], owner_map, replicas, head_size
        )
        weight_list.append(refreshed)
        token_rows = hidden[layer_index].reshape(seq_dev * steps, local_rows)
        partial_value = (
            jnp.dot(token_rows, refreshed, preferred_element_type=jnp.float32) * width_scale
        )
        projected = lax.psum(partial_value, "tensor")
        projected = projected + key_value_bias[layer_index].astype(jnp.float32)[None, :]
        is_key = jnp.arange(pair_count) % 2 == 0
        key_values = rotate(projected.reshape(-1, pair_count, head_size), positions, is_key).astype(
            jnp.bfloat16
        )
        key_values = key_values.reshape(seq_dev, steps, kv_heads, 2, head_size)
        highest, denominator, summed = partial_attention(
            queries[layer_index],
            key_cache[layer_index],
            value_cache[layer_index],
            key_values[:, :, :, 0, :],
            key_values[:, :, :, 1, :],
            lengths,
            tensor_index,
        )
        highest, denominator, summed = combined_all(
            (highest, denominator, summed), "tensor", joined
        )
        denominator = lax.dynamic_slice_in_dim(denominator, tensor_index * own_heads, own_heads, 2)
        summed = lax.dynamic_slice_in_dim(summed, tensor_index * own_heads, own_heads, 2)
        output_list.append((summed / denominator[..., None]).astype(jnp.bfloat16))
    return (jnp.stack(weight_list), jnp.stack(output_list))


def solution(mesh):
    in_specs = (
        P(None, "replica", None, "tensor"),
        P(None, "tensor", None),
        P(None, "tensor", "replica"),
        P(None, "tensor", "replica"),
        P(),
        P(),
        P(None, "replica", None, None, None),
        P(None, "replica", "tensor", None, None),
        P(None, "replica", "tensor", None, None),
        P("replica"),
    )
    out_specs = (P(None, "tensor", None), P(None, "replica", None, "tensor", None))
    return jax.shard_map(
        on_device, mesh=mesh, in_specs=in_specs, out_specs=out_specs, check_vma=False
    )
```

profile of v0, /device:TPU:2, one launch (start us, length us, event | category | flops | bytes accessed | tf_op | source)
XLA Modules:
  0.0 533.0 jit_solution(14759775461621419880)
XLA Ops:
  10.7 23.6 %all-gather.1 = bf16[1,512,16]{1,0,2:T(2,128)(2,1)S(1)} all-gather(bf16[1,512,1]{1,0,2:T(2,128)(2,1)S(1)} %get-tuple-element.428), channel_id=3, replica_groups=mesh['replica'=16,'tensor'=16] {'replica'}, dimensions={2}, use_global_device_ids=true | all-gather | bytes 17408 | tf_op jit(solution)/shard_map/all_gather | solution.py:141
  34.3 19.4 %all-gather.3 = bf16[1,512,16]{1,0,2:T(2,128)(2,1)S(1)} all-gather(bf16[1,512,1]{1,0,2:T(2,128)(2,1)S(1)} %get-tuple-element.429), channel_id=5, replica_groups=mesh['replica'=16,'tensor'=16] {'replica'}, dimensions={2}, use_global_device_ids=true | all-gather | bytes 17408 | tf_op jit(solution)/shard_map/all_gather | solution.py:141
  55.5 4.8 fusion.66
  60.4 2.9 copy.151
  63.2 2.8 copy.118
  66.1 3.9 copy.153
  70.0 4.2 copy.130
  75.1 2.8 fusion.68
  77.9 1.3 fusion.73
  79.2 1.2 fusion.67
  80.4 3.9 copy.110
  84.4 3.8 gather_fusion
  88.2 31.4 %all-gather.15.cloned.1.call-done = bf16[1,512,2048]{1,2,0:T(8,128)(2,1)} async-done(((bf16[1,512,128]{1,2,0:T(8,128)(2,1)}), bf16[1,512,2048]{1,2,0:T(8,128)(2,1)}) %all-gather.15.cloned.1.call-update) | async-done | bytes 2097168 | tf_op jit(solution)/shard_map/all_gather | solution.py:140
  119.6 3.9 copy.114
  123.5 3.7 gather_fusion.2
  127.3 10.0 %add_convert_fusion.1 = (bf16[512,16,128]{2,0,1:T(8,128)(2,1)}, f32[512,16,128]{2,0,1:T(8,128)}, f32[512,16,128]{2,0,1:T(8,128)}, bf16[512,16,128]{2,0,1:T(8,128)(2,1)}) fusion(f32[512,16,128]{2,0,1:T(8,128)} %copy.118, f32[512,16]{0,1:T(8,128)S(1)} %get-tuple-element.436, bf16[16,512,128]{2,1,0:T(8,128)(2,1)} %gather_fusion, ...), kind=kLoop, calls=%fused_computation.30 | loop fusion | flops 10485760 | bytes 25231376 | tf_op jit(solution)/shard_map/convert_element_type | solution.py:51
  137.2 3.9 copy.131
  141.2 4.0 copy.119
  145.1 3.0 fusion.12
  148.2 1.3 fusion.13
  149.5 128.8 %all-reduce.3.cloned.1.call-done = (f32[4,2048]{1,0:T(4,128)}, f32[4,2048]{1,0:T(4,128)}) async-done(((f32[4,2048]{1,0:T(4,128)}, f32[4,2048]{1,0:T(4,128)}), (f32[4,2048]{1,0:T(4,128)}, f32[4,2048]{1,0:T(4,128)})) %all-reduce.3.cloned.1.call-update) | async-done | bytes 65552 | tf_op jit(solution)/shard_map/psum | solution.py:151
  280.1 1.8 fusion.21
  282.8 2.5 fusion.71
  285.3 5.3 %copy.111 = f32[512,16,128]{0,2,1:T(8,128)} copy(f32[512,16,128]{2,0,1:T(8,128)} %get-tuple-element.409) | data formatting | bytes 8388608 | tf_op jit(solution)/shard_map/mul | solution.py:48
  290.7 5.3 %copy.115 = f32[512,16,128]{0,2,1:T(8,128)} copy(f32[512,16,128]{2,0,1:T(8,128)} %get-tuple-element.434) | data formatting | bytes 8388608 | tf_op jit(solution)/shard_map/mul | solution.py:48
  296.0 5.5 %fusion.10 = (bf16[1,512,2048]{1,2,0:T(8,128)(2,1)S(1)}, bf16[1,512,2048]{1,2,0:T(8,128)(2,1)S(1)}) fusion(f32[512,16,128]{0,2,1:T(8,128)} %copy.115, bf16[1,512,2048]{1,2,0:T(8,128)(2,1)} %copy.153, f32[512,16,128]{0,2,1:T(8,128)} %copy.111, bf16[1,512,2048]{1,2,0:T(8,128)(2,1)S(1)} %copy.151), kind=kLoop, calls=%fused_computation.26 | loop fusion | flops 6291456 | bytes 16777216 | tf_op jit(solution)/shard_map/convert_element_type | solution.py:51
  301.5 2.4 pad_maximum_fusion
  304.0 6.3 %copy.140 = bf16[2,512,2048]{2,1,0:T(8,128)(2,1)} copy(bf16[2,512,2048]{1,2,0:T(8,128)(2,1)} %pad_maximum_fusion) | data formatting | bytes 8388608
  313.0 31.2 %all_gather.35 = f32[16,1,4,64]{3,2,1,0:T(4,128)S(1)} all-gather(f32[1,1,4,64]{3,2,1,0:T(4,128)S(1)} %add.285), channel_id=1, replica_groups=mesh['replica'=16,'tensor'=16] {'tensor'}, dimensions={0}, use_global_device_ids=true | all-gather | bytes 17408 | tf_op jit(solution)/shard_map/all_gather | solution.py:13
  344.1 30.3 %all_gather.34 = f32[16,1,4,64]{3,2,1,0:T(4,128)S(1)} all-gather(f32[1,1,4,64]{3,2,1,0:T(4,128)S(1)} %max.59), channel_id=1, replica_groups=mesh['replica'=16,'tensor'=16] {'tensor'}, dimensions={0}, use_global_device_ids=true | all-gather | bytes 17408 | tf_op jit(solution)/shard_map/all_gather | solution.py:13
  374.5 31.2 %all_gather.38 = f32[16,1,4,64]{3,2,1,0:T(4,128)S(1)} all-gather(f32[1,1,4,64]{3,2,1,0:T(4,128)S(1)} %add.297), channel_id=1, replica_groups=mesh['replica'=16,'tensor'=16] {'tensor'}, dimensions={0}, use_global_device_ids=true | all-gather | bytes 17408 | tf_op jit(solution)/shard_map/all_gather | solution.py:13
  405.7 30.1 %all_gather.37 = f32[16,1,4,64]{3,2,1,0:T(4,128)S(1)} all-gather(f32[1,1,4,64]{3,2,1,0:T(4,128)S(1)} %max.61), channel_id=1, replica_groups=mesh['replica'=16,'tensor'=16] {'tensor'}, dimensions={0}, use_global_device_ids=true | all-gather | bytes 17408 | tf_op jit(solution)/shard_map/all_gather | solution.py:13
  436.8 17.3 %while.38 = (s32[]{:T(128)}, f32[1,4,64]{2,1,0:T(4,128)S(1)}, f32[1,4,64]{2,1,0:T(4,128)S(1)}, f32[1,4,64,128]{3,2,1,0:T(8,128)S(1)}, f32[16,1,4,64]{3,2,1,0:T(4...) while((s32[]{:T(128)}, f32[1,4,64]{2,1,0:T(4,128)S(1)}, ...), condition=%wide.region_6.9_spmd, body=%wide.region_5.8_spmd.sunk | while | flops 100101 | bytes 408731 | solution.py:18
  436.8 1.1 fusion.85
  438.0 1.1 fusion.85
  439.1 1.1 fusion.85
  440.3 1.1 fusion.85
  441.4 1.1 fusion.85
  442.6 1.1 fusion.85
  443.7 1.1 fusion.85
  444.9 1.1 fusion.85
  446.0 1.1 fusion.85
  447.2 1.1 fusion.85
  448.4 1.1 fusion.85
  449.5 1.1 fusion.85
  450.7 1.1 fusion.85
  451.8 1.1 fusion.85
  453.0 1.1 fusion.85
  454.1 53.3 %all-gather.11.cloned.1.call-done = f32[16,1,4,64,128]{4,3,2,1,0:T(8,128)} async-done(((f32[1,1,4,64,128]{4,3,2,1,0:T(8,128)}), f32[16,1,4,64,128]{4,3,2,1,0:T(8,128)}) %all-gather.11.cloned.1.call-update) | async-done | bytes 2097168 | tf_op jit(solution)/shard_map/all_gather | solution.py:13
  508.3 17.3 %while.39 = (s32[]{:T(128)}, f32[1,4,64]{2,1,0:T(4,128)S(1)}, f32[1,4,64]{2,1,0:T(4,128)S(1)}, f32[1,4,64,128]{3,2,1,0:T(8,128)S(1)}, f32[16,1,4,64]{3,2,1,0:T(4...) while((s32[]{:T(128)}, f32[1,4,64]{2,1,0:T(4,128)S(1)}, ...), condition=%wide.region_13.16_spmd, body=%wide.region_12.15_spmd.sunk | while | flops 100101 | bytes 408731 | solution.py:18
  508.3 1.1 fusion.88
  509.5 1.1 fusion.88
  510.6 1.1 fusion.88
  511.8 1.1 fusion.88
  512.9 1.1 fusion.88
  514.1 1.1 fusion.88
  515.2 1.1 fusion.88
  516.4 1.1 fusion.88
  517.5 1.1 fusion.88
  518.7 1.1 fusion.88
  519.8 1.1 fusion.88
  521.0 1.1 fusion.88
  522.1 1.1 fusion.88
  523.3 1.1 fusion.88
  (184 shorter events, 16.0 us)
Async XLA Ops:
  7.2 73.3 %all-gather.13.cloned.1.call-start = ((), (), s32[]{:S(2)}) async-start(), calls=%async_computation.2 | async-start | bytes 2228224 | tf_op jit(solution)/shard_map/all_gather | solution.py:140
  9.0 110.6 %all-gather.15.cloned.1.call-start = ((), (), s32[]{:S(2)}) async-start(), calls=%async_computation.3 | async-start | bytes 2228224 | tf_op jit(solution)/shard_map/all_gather | solution.py:140
  9.8 268.5 %all-reduce.3.cloned.1.call-start = ((), (), s32[]{:S(2)}) async-start(), calls=%async_computation.4 | async-start | bytes 131072 | tf_op jit(solution)/shard_map/psum | solution.py:151
  70.0 4.9 copy-start.7
  70.0 5.1 copy-start.4
  75.1 4.1 copy-start.3
  79.2 1.2 copy-start.5
  141.2 4.0 copy-start.6
  145.1 3.0 copy-start
  149.4 286.4 %all-gather.9.cloned.1.call-start = ((), (), s32[]{:S(2)}) async-start(), calls=%async_computation | async-start | bytes 2228224 | tf_op jit(solution)/shard_map/all_gather | solution.py:13
  282.6 224.8 %all-gather.11.cloned.1.call-start = ((), (), s32[]{:S(2)}) async-start(), calls=%async_computation.1 | async-start | bytes 2228224 | tf_op jit(solution)/shard_map/all_gather | solution.py:13
  303.9 6.4 %copy-start.1 = (f32[1,4,8,8,512]{4,3,1,2,0:T(8,128)S(1)}, f32[1,4,8,8,512]{4,3,1,2,0:T(8,128)}, u32[]{:S(2)}) copy-start(f32[1,4,8,8,512]{4,3,1,2,0:T(8,128)} %get-tuple-element.443) | copy-start | bytes 1572868
  303.9 7.5 %copy-start.2 = (f32[1,4,8,8,512]{4,3,1,2,0:T(8,128)S(1)}, f32[1,4,8,8,512]{4,3,1,2,0:T(8,128)}, u32[]{:S(2)}) copy-start(f32[1,4,8,8,512]{4,3,1,2,0:T(8,128)} %get-tuple-element.439) | copy-start | bytes 1572868
Sparse Core Ops, SparseCore 0:
  10.8 54.6 all-gather.12
  68.2 51.4 all-gather.14
  149.6 128.6 all-reduce.2
  282.7 70.0 all-gather.8
  435.9 71.3 all-gather.10
where the time goes:
time: 536 us; the launch traced here: 533 us
  waiting for transfers between devices  214 us (40%)
  blocking collectives  166 us (31%)
  local copies, waits for them, and re-layouts  71.2 us (13%)
  other arithmetic  54.5 us (10%)
  between operations  14.8 us (3%)
  matrix products  11.5 us (2%)
    psum x1, waiting for transfers between devices, on_device(): projected = lax.psum(partial_value, 'tensor')  129 us
    all_gather x4, blocking collectives, combined_all(): gathered = jax.tree.map(lambda a: lax.all_gather(a, axis), part)  123 us
    all_gather x2, waiting for transfers between devices, combined_all(): gathered = jax.tree.map(lambda a: lax.all_gather(a, axis), part)  53.3 us
    all_gather x2, blocking collectives, on_device(): lax.all_gather(scales[layer_index], 'replica', axis=1, tiled=True)  43 us
    add x30, other arithmetic, joined(): summed_a * factor_a[..., None] + summed_b * factor_b[..., None]  32.2 us
    all_gather x2, waiting for transfers between devices, on_device(): lax.all_gather(delta_codes[layer_index], 'replica', axis=1, tiled=True)  31.5 us
    convert_element_type x2, other arithmetic, apply_delta(): (resident_rows.astype(jnp.float32) + delta_full.reshape(local_rows, width...  15.5 us
    unnamed x25, local copies, waits for them, and re-layouts  14.7 us
  transfers between devices with their start and end apart: 5, of which 3 were waited for; matrix products, arithmetic and copies ran while one was open for 16% of the time, Pallas kernels for 0%

commit v1 on v0

v1 whole, which is shorter than its diff:
```python
import functools
import math

import jax
import jax.numpy as jnp
import numpy as np
from jax import lax
from jax.experimental import pallas as pl
from jax.experimental.pallas import tpu as pltpu
from jax.sharding import PartitionSpec as P

MESH = pl.DeviceIdType.MESH
ROPE_BASE = 1000000.0
MIB = 1 << 20
NEG = -1e30

LAYERS = 2
STEPS = 4
ROWS = 512
HD = 128
SLOTS = 16
PEERS = 16
HEADS = 64
KVH = 8
QROWS = STEPS * HEADS
OWN = QROWS // PEERS
SPOTS = 512
COLS = SPOTS * KVH
WIDE = 512
CHUNKS = 4
HALF = ROWS * LAYERS // CHUNKS
EXP_SCALE = HD**-0.5 * math.log2(math.e)


def place():
    replica = lax.axis_index("replica")
    return replica // 8, (replica // 2) % 4, replica % 2, lax.axis_index("tensor")


def slot_of(xh, y, c):
    return (xh * 4 + y) * 2 + c


def gather_kernel(
    map_hbm, len_ref, hid_hbm, res_hbm, code_hbm, scale_hbm, bias_hbm, inv_hbm, q_hbm, k_hbm, v_hbm,
    gat, out_ref,
    map_ref, hid_ref, res, code_ref, scale_ref, bias_ref, inv_ref, q_ref, kbuf, vbuf, qp, sbuf, top, total, acc, asend, arecv, proj, psend, precv,
    load_sem, r_sem, own_sem, y2_sem, cross_sem, far_sem, sib_sem,
    as_sem, ar_sem, ps_sem, pr_sem,
):
    xh, y, c, t = place()
    me = slot_of(xh, y, c)

    pairs = [
        (map_hbm, map_ref), (scale_hbm, scale_ref), (code_hbm, code_ref), (res_hbm, res),
        (q_hbm, q_ref), (k_hbm, kbuf), (v_hbm, vbuf),
        (hid_hbm, hid_ref), (bias_hbm, bias_ref), (inv_hbm, inv_ref),
    ]
    loads = [pltpu.make_async_copy(a, b, load_sem.at[i]) for i, (a, b) in enumerate(pairs)]
    for load in loads:
        load.start()

    def device(x2, y2, c2):
        return (slot_of(x2, y2, c2), t)

    y_up, y_down = (y + 1) % 4, (y + 3) % 4
    y_far = (y + 2) % 4
    to_up, to_down = device(xh, y_up, c), device(xh, y_down, c)
    to_x, to_sib = device(1 - xh, y, c), device(xh, y, 1 - c)

    barrier = pltpu.get_barrier_semaphore()
    for partner in (to_up, to_down, to_x, to_sib):
        pl.semaphore_signal(barrier, inc=1, device_id=partner, device_id_type=MESH)

    def greet(k, carry):
        pl.semaphore_signal(barrier, inc=1, device_id=(me, (t + k) % PEERS), device_id_type=MESH)
        return carry

    lax.fori_loop(1, PEERS, greet, 0)

    loads[0].wait()
    group = jnp.int32(0)
    for g in range(SLOTS):
        group = group + jnp.where(map_ref[g] == me, g, 0)
    for load in loads[1:4]:
        load.wait()
    group_all = jnp.broadcast_to(group.astype(jnp.float32), (HD, HD)).astype(jnp.bfloat16)
    for layer in range(LAYERS):
        for part in range(ROWS // HD):
            rows = pl.ds(part * HD, HD)
            line = scale_ref[pl.ds(layer, 1), rows].astype(jnp.float32)
            column = jnp.transpose(jnp.broadcast_to(line, (HD, HD)))
            code = code_ref[layer, rows, :].astype(jnp.float32)
            base = res[layer, rows, :HD]
            for g in range(1, SLOTS):
                base = jnp.where(group_all == g, res[layer, rows, g * HD : (g + 1) * HD], base)
            base = base.astype(jnp.float32)
            gat[me, layer, rows, :] = (base + code * column).astype(jnp.bfloat16)

    pl.semaphore_wait(barrier, PEERS - 1 + 4)

    def piece(slot, j):
        return gat.at[slot, j // 2, pl.ds(pl.multiple_of((j % 2) * HALF, HALF), HALF), :]

    def send(slot, j, sem, target):
        return pltpu.make_async_remote_copy(
            src_ref=piece(slot, j), dst_ref=piece(slot, j), send_sem=sem,
            recv_sem=r_sem.at[slot, j], device_id=target, device_id_type=MESH,
        )

    def arrived(slot, j):
        send(slot, j, r_sem.at[slot, j], to_sib).wait_recv()

    def loop(low, high, body):
        def step(j, carry):
            body(j)
            return carry

        lax.fori_loop(low, high, step, 0)

    s_up, s_down = slot_of(xh, y_up, c), slot_of(xh, y_down, c)
    s_far, s_x = slot_of(xh, y_far, c), slot_of(1 - xh, y, c)
    x_up, x_down = slot_of(1 - xh, y_up, c), slot_of(1 - xh, y_down, c)
    x_far = slot_of(1 - xh, y_far, c)

    def own_copies(j):
        return [
            send(me, j, own_sem.at[0, j], to_up),
            send(me, j, own_sem.at[1, j], to_down),
            send(me, j, own_sem.at[2, j], to_x),
            send(me, j, own_sem.at[3, j], to_sib),
        ]

    def onward(j):
        up = 1 - 2 * (j % 2)
        return slot_of(xh, (y + 4 - up) % 4, c), device(xh, (y + 4 + up) % 4, c)

    def y2_copy(j):
        slot, target = onward(j)
        return send(slot, j, y2_sem.at[j], target)

    def cross_copies(j):
        return [send(s_x, j, cross_sem.at[0, j], to_up), send(s_x, j, cross_sem.at[1, j], to_down)]

    def far_copy(j):
        return send(s_far, j, far_sem.at[j], to_x)

    sib_slots = [s_up, s_down, s_x, s_far, x_up, x_down, x_far]

    def sib_copy(i, j):
        return send(sib_slots[i], j, sib_sem.at[i, j], to_sib)

    def own_step(j):
        for copy in own_copies(j):
            copy.start()

    loop(0, CHUNKS, own_step)

    for load in loads[4:5]:
        load.wait()
    row = lax.broadcasted_iota(jnp.int32, (QROWS, QROWS), 0)
    col = lax.broadcasted_iota(jnp.int32, (QROWS, QROWS), 1)
    source = ((row // STEPS) % STEPS) * HEADS + (row // OWN) * STEPS + row % STEPS
    pick = jnp.where(col == source, 1.0, 0.0).astype(jnp.bfloat16)
    for layer in range(LAYERS):
        qp[layer] = jnp.dot(pick, q_ref[layer], preferred_element_type=jnp.float32).astype(
            jnp.bfloat16
        )
    length = len_ref[0]
    limit = (length - t * SPOTS) * KVH
    lanes = lax.broadcasted_iota(jnp.int32, (1, WIDE), 1)
    lane = lax.broadcasted_iota(jnp.int32, (QROWS, HD), 1)

    def scores(layer):
        top[...] = jnp.full((QROWS, HD), NEG, jnp.float32)

        def body(n):
            first = pl.multiple_of(n * WIDE, WIDE)
            s = lax.dot_general(
                qp[layer], kbuf[layer, pl.ds(first, WIDE), :], (((1,), (1,)), ((), ())),
                preferred_element_type=jnp.float32,
            )
            within = lanes + first < limit
            for g in range(KVH):
                rows = slice(g * 32, g * 32 + 32)
                bias = jnp.where(within & (lanes % KVH == g), 0.0, NEG)
                s_g = s[rows] + bias
                sbuf[rows, pl.ds(first, WIDE)] = s_g
                high = top[rows]
                for i in range(WIDE // HD):
                    high = jnp.maximum(high, s_g[:, i * HD : (i + 1) * HD])
                top[rows] = high

        loop(0, COLS // WIDE, body)
        top[...] = jnp.broadcast_to(jnp.max(top[...], axis=1, keepdims=True), (QROWS, HD))

    def values(layer):
        total[...] = jnp.zeros((QROWS, HD), jnp.float32)
        acc[...] = jnp.zeros((QROWS, HD), jnp.float32)

        def body(n):
            first = pl.multiple_of(n * WIDE, WIDE)
            high = top[...]
            added = total[...]
            parts = []
            for i in range(WIDE // HD):
                e = jnp.exp2((sbuf[:, pl.ds(first + i * HD, HD)] - high) * EXP_SCALE)
                added = added + e
                parts.append(e.astype(jnp.bfloat16))
            total[...] = added
            weights = jnp.concatenate(parts, axis=1)
            acc[...] += jnp.dot(
                weights, vbuf[layer, pl.ds(first, WIDE), :], preferred_element_type=jnp.float32
            )

        loop(0, COLS // WIDE, body)
        asend[:, layer * OWN : (layer + 1) * OWN, :] = acc[...].reshape(PEERS, OWN, HD)
        whole = jnp.sum(total[...], axis=1, keepdims=True)
        before = asend[:, 2 * OWN :, :].reshape(QROWS, HD) if layer else jnp.zeros((QROWS, HD))
        kept = jnp.where(lane == 2 * layer, top[...], before)
        kept = jnp.where(lane == 2 * layer + 1, jnp.broadcast_to(whole, (QROWS, HD)), kept)
        asend[:, 2 * OWN :, :] = kept.reshape(PEERS, OWN, HD)

    def near_step(j):
        slot, _ = onward(j)
        other = slot_of(xh, (y + 4 + 1 - 2 * (j % 2)) % 4, c)
        arrived(slot, j)
        y2_copy(j).start()
        arrived(s_x, j)
        for copy in cross_copies(j):
            copy.start()
        arrived(other, j)
        for i in range(3):
            sib_copy(i, j).start()

    loads[5].wait()
    scores(0)
    loads[6].wait()
    values(0)
    loop(0, 2, near_step)
    scores(1)
    values(1)
    loop(2, CHUNKS, near_step)

    def peer_copy(src, dst, s_sem, rr_sem, k):
        target = (t + k) % PEERS
        return pltpu.make_async_remote_copy(
            src_ref=src(target), dst_ref=dst.at[t], send_sem=s_sem.at[target],
            recv_sem=rr_sem.at[t], device_id=(me, target), device_id_type=MESH,
        )

    def peer_arrived(src, dst, s_sem, rr_sem, k):
        other = (t + k) % PEERS
        pltpu.make_async_remote_copy(
            src_ref=src(other), dst_ref=dst.at[other], send_sem=s_sem.at[other],
            recv_sem=rr_sem.at[other], device_id=(me, other), device_id_type=MESH,
        ).wait_recv()

    attention = (lambda target: asend.at[target], arecv, as_sem, ar_sem)
    project = (lambda target: psend.at[target // 2], precv, ps_sem, pr_sem)
    loop(1, PEERS, lambda k: peer_copy(*attention, k).start())
    arecv[t] = asend[t]

    for load in loads[7:]:
        load.wait()
    hidden = [hid_ref[layer, 0] for layer in range(LAYERS)]

    def multiply(slot, layer):
        proj[slot, pl.ds(layer * STEPS, STEPS), :] = jnp.dot(
            hidden[layer], gat[slot, layer], preferred_element_type=jnp.float32
        )

    def far_step(j):
        arrived(s_far, j)
        far_copy(j).start()
        sib_copy(3, j).start()

    def settle(slots, layer):
        for slot in slots:
            multiply(slot, layer)

    def flip(slot):
        return slot + 1 - 2 * c

    near = [s_up, s_down, s_x]
    loop(0, 2, far_step)
    for slot in [me]:
        for layer in range(LAYERS):
            multiply(slot, layer)
    for slot in [me] + near:
        loop(0, CHUNKS, lambda j, slot=slot: arrived(flip(slot), j))
    for layer in range(LAYERS):
        settle(near, layer)
        settle([flip(slot) for slot in [me] + near], layer)
    loop(2, CHUNKS, far_step)

    def late_step(j):
        arrived(x_up, j)
        sib_copy(4, j).start()
        arrived(x_down, j)
        sib_copy(5, j).start()
        arrived(x_far, j)
        sib_copy(6, j).start()

    loop(0, 2, late_step)

    loop(1, PEERS, lambda k: peer_arrived(*attention, k))
    joined = []
    for layer in range(LAYERS):
        highs = [arecv[p, 2 * OWN :, 2 * layer : 2 * layer + 1] for p in range(PEERS)]
        high = functools.reduce(jnp.maximum, highs)
        whole = jnp.zeros((OWN, 1), jnp.float32)
        summed = jnp.zeros((OWN, HD), jnp.float32)
        for p in range(PEERS):
            factor = jnp.exp2((highs[p] - high) * EXP_SCALE)
            whole = whole + factor * arecv[p, 2 * OWN :, 2 * layer + 1 : 2 * layer + 2]
            summed = summed + factor * arecv[p, layer * OWN : (layer + 1) * OWN, :]
        joined.append((high, whole, summed))

    turn_row = lax.broadcasted_iota(jnp.int32, (LAYERS * STEPS, HD), 0)
    turn_lane = lax.broadcasted_iota(jnp.int32, (LAYERS * STEPS, HD), 1)
    angle = (length + turn_row % STEPS).astype(jnp.float32) * inv_ref[...]
    cosine = jnp.cos(angle)
    sine = jnp.where(turn_lane < HD // 2, -1.0, 1.0) * jnp.sin(angle)

    far = [s_far, x_up, x_down, x_far]
    for slot in far:
        loop(0, 2, lambda j, slot=slot: arrived(flip(slot), j))
    settle(far + [flip(slot) for slot in far], 0)
    loop(2, CHUNKS, late_step)
    settle(far, 1)
    for slot in far:
        loop(2, CHUNKS, lambda j, slot=slot: arrived(flip(slot), j))
    settle([flip(slot) for slot in far], 1)

    for g in range(SLOTS):
        slot_all = jnp.broadcast_to(map_ref[g], (LAYERS * STEPS, HD))
        line = proj[0]
        for slot in range(1, SLOTS):
            line = jnp.where(slot_all == slot, proj[slot], line)
        psend[g // 2, (g % 2) * 8 : (g % 2) * 8 + 8, :] = line
    loop(1, PEERS, lambda k: peer_copy(*project, k).start())
    precv[t] = psend[t // 2]
    head = t // 2
    bias = bias_ref[:, pl.ds(pl.multiple_of(head * 2 * HD, 2 * HD), 2 * HD)].astype(jnp.float32)
    loop(1, PEERS, lambda k: peer_arrived(*project, k))
    projected = precv[0]
    for p in range(1, PEERS):
        projected = projected + precv[p]
    projected = projected * (ROWS * PEERS) ** -0.5

    def biased(kind):
        part = projected[kind * 8 : kind * 8 + 8]
        line = [
            jnp.broadcast_to(bias[layer : layer + 1, kind * HD : (kind + 1) * HD], (8, HD))
            for layer in range(LAYERS)
        ]
        return part + jnp.where(turn_row < STEPS, line[0], line[1])

    key = biased(0)
    key = (key * cosine + pltpu.roll(key, HD // 2, 1) * sine).astype(jnp.bfloat16)
    value = biased(1).astype(jnp.bfloat16)
    row = lax.broadcasted_iota(jnp.int32, (OWN, LAYERS * STEPS), 0)
    col = lax.broadcasted_iota(jnp.int32, (OWN, LAYERS * STEPS), 1)
    for layer in range(LAYERS):
        query = qp[layer, pl.ds(pl.multiple_of(t * OWN, OWN), OWN), :]
        s = lax.dot_general(
            query, key, (((1,), (1,)), ((), ())), preferred_element_type=jnp.float32
        )
        allowed = (col // STEPS == layer) & (col % STEPS <= row // STEPS)
        s = jnp.where(allowed, s, NEG)
        high, whole, summed = joined[layer]
        top_all = jnp.maximum(high, jnp.max(s, axis=1, keepdims=True))
        e = jnp.exp2((s - top_all) * EXP_SCALE)
        factor = jnp.exp2((high - top_all) * EXP_SCALE)
        whole = whole * factor + jnp.sum(e, axis=1, keepdims=True)
        summed = summed * factor + jnp.dot(
            e.astype(jnp.bfloat16), value, preferred_element_type=jnp.float32
        )
        result = (summed / whole).astype(jnp.bfloat16)
        for step in range(STEPS):
            out_ref[layer, 0, step] = result[step * 4 : step * 4 + 4]

    def sent(j):
        for copy in own_copies(j) + cross_copies(j) + [y2_copy(j), far_copy(j)]:
            copy.wait_send()
        for i in range(len(sib_slots)):
            sib_copy(i, j).wait_send()

    loop(0, CHUNKS, sent)
    loop(1, PEERS, lambda k: peer_copy(*attention, k).wait_send())
    loop(1, PEERS, lambda k: peer_copy(*project, k).wait_send())


def place_kernel(map_ref, gat, part, out_hbm, part_out, sem):
    copies = []
    for group in range(SLOTS):
        for layer in range(LAYERS):
            copy = pltpu.make_async_copy(
                gat.at[map_ref[group], layer],
                out_hbm.at[layer, :, pl.ds(group * HD, HD)],
                sem.at[group, layer],
            )
            copy.start()
            copies.append(copy)
    part_out[...] = part[...]
    for copy in copies:
        copy.wait()


def on_device(
    hidden, resident, delta_codes, scales, owner_map, key_value_bias, queries, key_cache,
    value_cache, lengths,
):
    inverse = (ROPE_BASE ** (-2.0 * np.arange(HD // 2) / HD)).astype(np.float32)
    inverse = jnp.asarray(np.concatenate([inverse, inverse])[None, :])
    smem = pl.BlockSpec(memory_space=pltpu.SMEM)
    vmem = pl.BlockSpec(memory_space=pltpu.VMEM)
    hbm = pl.BlockSpec(memory_space=pltpu.HBM)
    anywhere = pl.BlockSpec(memory_space=pl.ANY)
    dma = pltpu.SemaphoreType.DMA
    f32, bf16 = jnp.float32, jnp.bfloat16
    part_shape = (LAYERS, 1, STEPS, HEADS // PEERS, HD)
    arrays = (
        owner_map, lengths, hidden, resident, delta_codes,
        scales.reshape(LAYERS, ROWS), key_value_bias, inverse,
        queries.reshape(LAYERS, QROWS, HD),
        key_cache.reshape(LAYERS, COLS, HD), value_cache.reshape(LAYERS, COLS, HD),
    )
    gathered, part = pl.pallas_call(
        gather_kernel,
        out_shape=(
            pltpu.VMEM((SLOTS, LAYERS, ROWS, HD), bf16),
            jax.ShapeDtypeStruct(part_shape, bf16),
        ),
        in_specs=[hbm, smem] + [hbm] * 9,
        out_specs=(vmem, vmem),
        scratch_shapes=[
            pltpu.SMEM((SLOTS,), jnp.int32),
            pltpu.VMEM((LAYERS, 1, STEPS, ROWS), bf16),
            pltpu.VMEM((LAYERS, ROWS, SLOTS * HD), bf16),
            pltpu.VMEM((LAYERS, ROWS, HD), bf16),
            pltpu.VMEM((LAYERS, ROWS), bf16),
            pltpu.VMEM((LAYERS, SLOTS * HD), bf16),
            pltpu.VMEM((1, HD), f32),
            pltpu.VMEM((LAYERS, QROWS, HD), bf16),
            pltpu.VMEM((LAYERS, COLS, HD), bf16),
            pltpu.VMEM((LAYERS, COLS, HD), bf16),
            pltpu.VMEM((LAYERS, QROWS, HD), bf16),
            pltpu.VMEM((QROWS, COLS), f32),
            pltpu.VMEM((QROWS, HD), f32),
            pltpu.VMEM((QROWS, HD), f32),
            pltpu.VMEM((QROWS, HD), f32),
            pltpu.VMEM((PEERS, 3 * OWN, HD), f32),
            pltpu.VMEM((PEERS, 3 * OWN, HD), f32),
            pltpu.VMEM((SLOTS, LAYERS * STEPS, HD), f32),
            pltpu.VMEM((PEERS // 2, 16, HD), f32),
            pltpu.VMEM((PEERS, 16, HD), f32),
            dma((10,)),
            dma((SLOTS, CHUNKS)),
            dma((4, CHUNKS)),
            dma((CHUNKS,)),
            dma((2, CHUNKS)),
            dma((CHUNKS,)),
            dma((7, CHUNKS)),
            dma((PEERS,)),
            dma((PEERS,)),
            dma((PEERS,)),
            dma((PEERS,)),
        ],
        compiler_params=pltpu.CompilerParams(
            collective_id=0, has_side_effects=True, vmem_limit_bytes=40 * MIB
        ),
    )(*(a if a.size == 1 else pltpu.with_memory_space_constraint(a, pltpu.HBM) for a in arrays))
    return pl.pallas_call(
        place_kernel,
        out_shape=(
            jax.ShapeDtypeStruct((LAYERS, ROWS, SLOTS * HD), bf16),
            jax.ShapeDtypeStruct(part_shape, bf16),
        ),
        in_specs=[smem, vmem, vmem],
        out_specs=(anywhere, vmem),
        scratch_shapes=[dma((SLOTS, LAYERS))],
        compiler_params=pltpu.CompilerParams(vmem_limit_bytes=16 * MIB),
    )(owner_map, gathered, part)


def solution(mesh):
    in_specs = (
        P(None, "replica", None, "tensor"),
        P(None, "tensor", None),
        P(None, "tensor", "replica"),
        P(None, "tensor", "replica"),
        P(),
        P(),
        P(None, "replica", None, None, None),
        P(None, "replica", "tensor", None, None),
        P(None, "replica", "tensor", None, None),
        P("replica"),
    )
    out_specs = (P(None, "tensor", None), P(None, "replica", None, "tensor", None))
    return jax.shard_map(
        on_device, mesh=mesh, in_specs=in_specs, out_specs=out_specs, check_vma=False
    )
```

time: 536 us -> 46.3 us (0.09)
  the two profiles are of different devices: /device:TPU:2 before, /device:TPU:1 now
where the time goes in v1:
time: 46.3 us; the launch traced here: 46.2 us
  Pallas kernels  44.9 us (97%)
  between operations  1.3 us (3%)
    pallas_call x1, Pallas kernels, on_device(): pl.pallas_call(gather_kernel, out_shape=(pltpu.VMEM((SLOTS, LAYERS, ROWS,...  41.5 us
    pallas_call x1, Pallas kernels, on_device(): pl.pallas_call(place_kernel, out_shape=(jax.ShapeDtypeStruct((LAYERS, ROW...  3.41 us

profile of v1, /device:TPU:1, one launch (start us, length us, event | category | flops | bytes accessed | tf_op | source)
XLA Modules:
  0.0 46.2 jit_solution(1569889564238628068)
XLA Ops:
  1.3 0.0 copy-start
  1.3 41.5 %shard_map.122 = (bf16[16,2,512,128]{3,2,1,0:T(8,128)(2,1)S(1)}, bf16[2,1,4,4,128]{4,3,2,1,0:T(4,128)(2,1)S(1)}) custom-call(s32[16]{0:T(128)} %map_ref.1, s32[1]{0:T(128)S(6)} %copy.13.len_ref, bf16[2,1,4,512]{3,2,1,0:T(4,128)(2,1)} %hid_hbm.1, bf16[2,512,2048]{2,1,0:T(8,128)(2,1)} %res_hbm.1, bf16[2,512,128]{2,1,0:T(8,128)(2,1)} %code_hbm.1, ...), custom_call_target="tpu_custom_call" | custom-call | tf_op jit(solution)/shard_map/pallas_call | solution.py:430
  42.8 0.0 copy-done
  42.8 3.4 %shard_map.123 = (bf16[2,512,2048]{2,1,0:T(8,128)(2,1)}, bf16[2,1,4,4,128]{4,3,2,1,0:T(4,128)(2,1)}) custom-call(s32[16]{0:T(128)S(1)} %copy-done, bf16[16,2,512,128]{3,2,1,0:T(8,128)(2,1)S(1)} %get-tuple-element.4.gat, bf16[2,1,4,4,128]{4,3,2,1,0:T(4,128)(2,1)S(1)} %get-tuple-element.5.part), custom_call_target="tpu_custom_call" | custom-call | tf_op jit(solution)/shard_map/pallas_call | solution.py:475
Async XLA Ops:
  1.3 41.5 %copy-start = (s32[16]{0:T(128)S(1)}, s32[16]{0:T(128)}, u32[]{:S(2)}) copy-start(s32[16]{0:T(128)} %map_ref.1) | copy-start | bytes 196

commit v2 on v1

v2 whole, which is shorter than its diff:
```python
import functools
import math

import jax
import jax.numpy as jnp
import numpy as np
from jax import lax
from jax.experimental import pallas as pl
from jax.experimental.pallas import tpu as pltpu
from jax.sharding import PartitionSpec as P

MESH = pl.DeviceIdType.MESH
ROPE_BASE = 1000000.0
MIB = 1 << 20
NEG = -1e30

LAYERS = 2
STEPS = 4
ROWS = 512
HD = 128
SLOTS = 16
PEERS = 16
HEADS = 64
KVH = 8
QROWS = STEPS * HEADS
OWN = QROWS // PEERS
SPOTS = 512
COLS = SPOTS * KVH
WIDE = 1024
CHIPS = 8
CHUNKS = 4
HALF = ROWS * LAYERS // CHUNKS
EXP_SCALE = HD**-0.5 * math.log2(math.e)


def place():
    replica = lax.axis_index("replica")
    return replica // 8, (replica // 2) % 4, replica % 2, lax.axis_index("tensor")


def slot_of(xh, y, c):
    return (xh * 4 + y) * 2 + c


def gather_kernel(
    map_hbm, len_ref, hid_hbm, res_hbm, code_hbm, scale_hbm, bias_hbm, inv_hbm, q_hbm, k_hbm, v_hbm,
    gat, out_ref, map_out,
    map_ref, hid_ref, res, code_ref, scale_ref, bias_ref, inv_ref, q_ref, kbuf, vbuf,
    hall, qp, sbuf, top, peak, total, acc, side, asend, arecv, part, proj, psend, precv,
    load_sem, r_sem, sib_r_sem, own_sem, y2_sem, cross_sem, far_sem, sib_sem,
    h_r_sem, h_sem, token_sem, as_sem, ar_sem, part_sem, part_r_sem, ps_sem, pr_sem,
):
    xh, y, c, t = place()
    me = slot_of(xh, y, c)

    pairs = [
        (map_hbm, map_ref), (scale_hbm, scale_ref), (code_hbm, code_ref), (res_hbm, res),
        (hid_hbm, hid_ref), (q_hbm, q_ref), (k_hbm, kbuf), (v_hbm, vbuf),
        (bias_hbm, bias_ref), (inv_hbm, inv_ref),
    ]
    loads = [pltpu.make_async_copy(a, b, load_sem.at[i]) for i, (a, b) in enumerate(pairs)]
    for load in loads:
        load.start()

    def loop(low, high, body):
        def step(j, carry):
            body(j)
            return carry

        lax.fori_loop(low, high, step, 0)

    def device(x2, y2, c2):
        return (slot_of(x2, y2, c2), t)

    y_up, y_down, y_far = (y + 1) % 4, (y + 3) % 4, (y + 2) % 4
    to_up, to_down = device(xh, y_up, c), device(xh, y_down, c)
    to_x, to_sib = device(1 - xh, y, c), device(xh, y, 1 - c)

    barrier = pltpu.get_barrier_semaphore()
    chip = xh * 4 + y
    pl.semaphore_signal(barrier, inc=1, device_id=to_sib, device_id_type=MESH)

    def chip_device(k):
        return (((chip + k) % CHIPS) * 2 + c, t)

    def greet_chip(k):
        pl.semaphore_signal(barrier, inc=1, device_id=chip_device(k), device_id_type=MESH)

    loop(1, CHIPS, greet_chip)

    def greet(k):
        pl.semaphore_signal(barrier, inc=1, device_id=(me, k), device_id_type=MESH)

    loop(t + 1, PEERS, greet)

    loads[0].wait()
    group = jnp.int32(0)
    for g in range(SLOTS):
        group = group + jnp.where(map_ref[g] == me, g, 0)
        map_out[g] = map_ref[g]
    for load in loads[1:5]:
        load.wait()
    group_all = jnp.broadcast_to(group.astype(jnp.float32), (HD, HD)).astype(jnp.bfloat16)
    for layer in range(LAYERS):
        for p in range(ROWS // HD):
            rows = pl.ds(p * HD, HD)
            line = scale_ref[pl.ds(layer, 1), rows].astype(jnp.float32)
            column = jnp.transpose(jnp.broadcast_to(line, (HD, HD)))
            code = code_ref[layer, rows, :].astype(jnp.float32)
            base = res[layer, rows, :HD]
            for g in range(1, SLOTS):
                base = jnp.where(group_all == g, res[layer, rows, g * HD : (g + 1) * HD], base)
            base = base.astype(jnp.float32)
            gat[me, layer, rows, :] = (base + code * column).astype(jnp.bfloat16)
    halves = [
        hid_ref[layer, 0, :, h * 256 : (h + 1) * 256].astype(jnp.float32)
        for h in range(2)
        for layer in range(LAYERS)
    ]
    hall[c, chip] = jnp.concatenate(halves, axis=0).astype(jnp.bfloat16)

    pl.semaphore_wait(barrier, CHIPS + t)

    def copy_of(src, dst, s_sem, rr_sem, target):
        return pltpu.make_async_remote_copy(
            src_ref=src, dst_ref=dst, send_sem=s_sem, recv_sem=rr_sem,
            device_id=target, device_id_type=MESH,
        )

    s_up, s_down = slot_of(xh, y_up, c), slot_of(xh, y_down, c)
    s_far, s_x = slot_of(xh, y_far, c), slot_of(1 - xh, y, c)
    x_up, x_down = slot_of(1 - xh, y_up, c), slot_of(1 - xh, y_down, c)
    x_far = slot_of(1 - xh, y_far, c)
    others = [s_up, s_down, s_x, s_far, x_up, x_down, x_far]

    def flip(slot):
        return slot + 1 - 2 * c

    def h_copy(k):
        return copy_of(
            hall.at[c, chip], hall.at[c, chip], h_sem.at[k], h_r_sem.at[chip], chip_device(k)
        )

    def h_arrived(k):
        other = (chip + k) % CHIPS
        copy_of(
            hall.at[c, other], hall.at[c, other], h_sem.at[k], h_r_sem.at[other], to_sib
        ).wait_recv()

    def h_sib(core):
        return copy_of(hall.at[core], hall.at[core], h_sem.at[0], h_r_sem.at[CHIPS], to_sib)

    def rows_of(slot, j, count):
        return gat.at[slot, j // 2, pl.ds(pl.multiple_of((j % 2) * HALF, HALF), HALF * count), :]

    def send(slot, j, sem, target):
        ref = rows_of(slot, j, 1)
        return copy_of(ref, ref, sem, r_sem.at[slot, j], target)

    def arrived(slot, j):
        send(slot, j, r_sem.at[slot, j], to_sib).wait_recv()

    def sib_copy(i, slot, layer):
        ref = gat.at[slot, layer]
        return copy_of(ref, ref, sib_sem.at[i, layer], sib_r_sem.at[slot, layer], to_sib)

    def sib_send(i, layer):
        sib_copy(i, others[i - 1] if i else me, layer).start()

    def own_copies(j):
        return [
            send(me, j, own_sem.at[0, j], to_up),
            send(me, j, own_sem.at[1, j], to_down),
            send(me, j, own_sem.at[2, j], to_x),
        ]

    def onward(j):
        up = 1 - 2 * (j % 2)
        return slot_of(xh, (y + 4 - up) % 4, c), device(xh, (y + 4 + up) % 4, c)

    def y2_copy(j):
        slot, target = onward(j)
        return send(slot, j, y2_sem.at[j], target)

    def cross_copies(j):
        return [send(s_x, j, cross_sem.at[0, j], to_up), send(s_x, j, cross_sem.at[1, j], to_down)]

    def far_copy(j):
        return send(s_far, j, far_sem.at[j], to_x)

    def y2_step(j):
        slot, _ = onward(j)
        arrived(slot, j)
        y2_copy(j).start()

    def cross_step(j):
        arrived(s_x, j)
        for copy in cross_copies(j):
            copy.start()

    loop(1, CHIPS, lambda k: h_copy(k).start())

    def own_step(j):
        for copy in own_copies(j):
            copy.start()

    loop(0, CHUNKS - 1, own_step)

    def answer(k):
        pl.semaphore_signal(token_sem, inc=1, device_id=(me, k), device_id_type=MESH)

    loop(0, t, answer)

    loads[5].wait()
    row = lax.broadcasted_iota(jnp.int32, (QROWS, QROWS), 0)
    col = lax.broadcasted_iota(jnp.int32, (QROWS, QROWS), 1)
    source = ((row // STEPS) % STEPS) * HEADS + (row // OWN) * STEPS + row % STEPS
    pick = jnp.where(col == source, 1.0, 0.0).astype(jnp.bfloat16)
    for layer in range(LAYERS):
        qp[layer] = jnp.dot(pick, q_ref[layer], preferred_element_type=jnp.float32).astype(
            jnp.bfloat16
        )
    length = len_ref[0]
    limit = (length - t * SPOTS) * KVH
    lanes = lax.broadcasted_iota(jnp.int32, (1, WIDE), 1)
    lane = lax.broadcasted_iota(jnp.int32, (QROWS, HD), 1)
    valid = lane % KVH == lax.broadcasted_iota(jnp.int32, (QROWS, HD), 0) // (QROWS // KVH)

    def scores(layer):
        top[...] = jnp.full((QROWS, HD), NEG, jnp.float32)
        for n in range(COLS // WIDE):
            first = n * WIDE
            s = lax.dot_general(
                qp[layer], kbuf[layer, first : first + WIDE, :], (((1,), (1,)), ((), ())),
                preferred_element_type=jnp.float32,
            )
            s = s + jnp.where(lanes + first < limit, 0.0, NEG)
            sbuf[:, first : first + WIDE] = s
            high = top[...]
            for i in range(WIDE // HD):
                high = jnp.maximum(high, s[:, i * HD : (i + 1) * HD])
            top[...] = high
        high = jnp.max(jnp.where(valid, top[...], NEG), axis=1, keepdims=True)
        peak[...] = jnp.broadcast_to(high, (QROWS, HD))
        top[...] = jnp.where(valid, high, -NEG)

    def values(layer):
        total[...] = jnp.zeros((QROWS, HD), jnp.float32)
        acc[...] = jnp.zeros((QROWS, HD), jnp.float32)
        for n in range(COLS // WIDE):
            first = n * WIDE
            high = top[...]
            added = total[...]
            pieces = []
            for i in range(WIDE // HD):
                e = jnp.exp2((sbuf[:, first + i * HD : first + (i + 1) * HD] - high) * EXP_SCALE)
                added = added + e
                pieces.append(e.astype(jnp.bfloat16))
            total[...] = added
            acc[...] += jnp.dot(
                jnp.concatenate(pieces, axis=1), vbuf[layer, first : first + WIDE, :],
                preferred_element_type=jnp.float32,
            )
        whole = jnp.broadcast_to(jnp.sum(total[...], axis=1, keepdims=True), (QROWS, HD))
        asend[:, layer * OWN : (layer + 1) * OWN, :] = (
            (acc[...] / whole).astype(jnp.bfloat16).reshape(PEERS, OWN, HD)
        )
        rest = peak[...] * EXP_SCALE + jnp.log(whole) * math.log2(math.e)
        kept = side[...] if layer else jnp.zeros((QROWS, HD), jnp.float32)
        for i in range(3):
            term = rest.astype(jnp.bfloat16).astype(jnp.float32)
            rest = rest - term
            kept = jnp.where(lane == 3 * layer + i, term, kept)
        side[...] = kept

    loads[6].wait()
    scores(0)
    loads[7].wait()
    values(0)
    own_step(CHUNKS - 1)
    for layer in range(LAYERS):
        sib_send(0, layer)
    loop(1, CHIPS, h_arrived)
    h_sib(c).start()
    scores(1)
    loop(0, 2, y2_step)
    h_sib(1 - c).wait_recv()

    rows8 = lax.broadcasted_iota(jnp.int32, (SLOTS, LAYERS * STEPS, HD), 1)
    product = []
    for layer in range(LAYERS):
        halves = [
            jnp.dot(
                hall[...].reshape(SLOTS * 16, 256), gat[me, layer, h * 256 : (h + 1) * 256, :],
                preferred_element_type=jnp.float32,
            ).reshape(SLOTS, 16, HD)
            for h in range(2)
        ]
        product.append(halves[0][:, :8] + halves[1][:, 8:])
    part[...] = jnp.where(rows8 < STEPS, product[0], product[1])

    def part_copy(k):
        target = (me + k) % SLOTS
        return copy_of(
            part.at[(target % 2) * CHIPS + target // 2], proj.at[me],
            part_sem.at[target], part_r_sem.at[me], (target, t),
        )

    def part_arrived(k):
        other = (me + k) % SLOTS
        copy_of(
            part.at[other], proj.at[other], part_sem.at[other], part_r_sem.at[other], to_sib
        ).wait_recv()

    loop(1, SLOTS, lambda k: part_copy(k).start())
    proj[me] = part[c * CHIPS + chip]

    values(1)
    asend[:, 2 * OWN :, :] = side[...].astype(jnp.bfloat16).reshape(PEERS, OWN, HD)
    loop(2, CHUNKS, y2_step)
    loop(0, 2, cross_step)

    def peer_copy(src, dst, s_sem, rr_sem, k):
        target = (t + k) % PEERS
        return copy_of(src(target), dst.at[t], s_sem.at[target], rr_sem.at[t], (me, target))

    def peer_arrived(src, dst, s_sem, rr_sem, k):
        other = (t + k) % PEERS
        copy_of(
            src(other), dst.at[other], s_sem.at[other], rr_sem.at[other], (me, other)
        ).wait_recv()

    attention = (lambda target: asend.at[target], arecv, as_sem, ar_sem)
    project = (lambda target: psend.at[target // 2], precv, ps_sem, pr_sem)
    loop(1, SLOTS, part_arrived)
    for g in range(SLOTS):
        slot_all = jnp.broadcast_to(map_ref[g], (LAYERS * STEPS, HD))
        line = proj[0]
        for slot in range(1, SLOTS):
            line = jnp.where(slot_all == slot, proj[slot], line)
        psend[g // 2, (g % 2) * 8 : (g % 2) * 8 + 8, :] = line
    precv[t] = psend[t // 2]
    arecv[t] = asend[t]

    def send_peers():
        pl.when(t < PEERS - 1)(lambda: pl.semaphore_wait(token_sem, PEERS - 1 - t))
        loop(1, PEERS, lambda k: peer_copy(*project, k).start())
        loop(1, PEERS, lambda k: peer_copy(*attention, k).start())

    pl.when(t >= PEERS // 2)(send_peers)
    loop(2, CHUNKS, cross_step)

    def opposite_step(j):
        arrived(slot_of(xh, (y + 4 + 1 - 2 * (j % 2)) % 4, c), j)

    def far_step(j):
        arrived(s_far, j)
        far_copy(j).start()

    loop(0, CHUNKS, far_step)
    pl.when(t < PEERS // 2)(send_peers)
    loop(0, CHUNKS, opposite_step)
    for layer in range(LAYERS):
        for i in range(4):
            sib_send(i + 1, layer)

    for load in loads[8:]:
        load.wait()
    turn_row = lax.broadcasted_iota(jnp.int32, (LAYERS * STEPS, HD), 0)
    turn_lane = lax.broadcasted_iota(jnp.int32, (LAYERS * STEPS, HD), 1)
    angle = (length + turn_row % STEPS).astype(jnp.float32) * inv_ref[...]
    cosine = jnp.cos(angle)
    sine = jnp.where(turn_lane < HD // 2, -1.0, 1.0) * jnp.sin(angle)
    head = t // 2
    bias = bias_ref[:, pl.ds(pl.multiple_of(head * 2 * HD, 2 * HD), 2 * HD)].astype(jnp.float32)

    for layer in range(LAYERS):
        for i, slot in ((5, x_up), (6, x_down), (7, x_far)):
            loop(2 * layer, 2 * layer + 2, lambda j, slot=slot: arrived(slot, j))
            sib_send(i, layer)

    loop(1, PEERS, lambda k: peer_arrived(*attention, k))
    joined = []
    sides = [arecv[p, 2 * OWN :, :].astype(jnp.float32) for p in range(PEERS)]
    for layer in range(LAYERS):
        logs = [sum(x[:, 3 * layer + i : 3 * layer + i + 1] for i in range(3)) for x in sides]
        high = functools.reduce(jnp.maximum, logs)
        whole = jnp.zeros((OWN, 1), jnp.float32)
        summed = jnp.zeros((OWN, HD), jnp.float32)
        for p in range(PEERS):
            factor = jnp.exp2(logs[p] - high)
            whole = whole + factor
            summed = summed + factor * arecv[p, layer * OWN : (layer + 1) * OWN, :].astype(jnp.float32)
        joined.append((high, whole, summed))

    loop(1, PEERS, lambda k: peer_arrived(*project, k))
    projected = precv[0]
    for p in range(1, PEERS):
        projected = projected + precv[p]
    projected = projected * (ROWS * PEERS) ** -0.5

    def biased(kind):
        lines = [
            jnp.broadcast_to(bias[layer : layer + 1, kind * HD : (kind + 1) * HD], (8, HD))
            for layer in range(LAYERS)
        ]
        return projected[kind * 8 : kind * 8 + 8] + jnp.where(turn_row < STEPS, lines[0], lines[1])

    key = biased(0)
    key = (key * cosine + pltpu.roll(key, HD // 2, 1) * sine).astype(jnp.bfloat16)
    value = biased(1).astype(jnp.bfloat16)
    row = lax.broadcasted_iota(jnp.int32, (OWN, LAYERS * STEPS), 0)
    col = lax.broadcasted_iota(jnp.int32, (OWN, LAYERS * STEPS), 1)
    for layer in range(LAYERS):
        query = qp[layer, pl.ds(pl.multiple_of(t * OWN, OWN), OWN), :]
        s = lax.dot_general(
            query, key, (((1,), (1,)), ((), ())), preferred_element_type=jnp.float32
        )
        allowed = (col // STEPS == layer) & (col % STEPS <= row // STEPS)
        s = jnp.where(allowed, s * EXP_SCALE, NEG)
        high, whole, summed = joined[layer]
        top_all = jnp.maximum(high, jnp.max(s, axis=1, keepdims=True))
        e = jnp.exp2(s - top_all)
        factor = jnp.exp2(high - top_all)
        whole = whole * factor + jnp.sum(e, axis=1, keepdims=True)
        summed = summed * factor + jnp.dot(
            e.astype(jnp.bfloat16), value, preferred_element_type=jnp.float32
        )
        result = (summed / whole).astype(jnp.bfloat16)
        for step in range(STEPS):
            out_ref[layer, 0, step] = result[step * 4 : step * 4 + 4]

    for i, slot in enumerate([me] + others):
        for layer in range(LAYERS):
            sib_copy(i, flip(slot), layer).wait_recv()
            sib_copy(i, slot, layer).wait_send()

    def sent(j):
        for copy in own_copies(j) + cross_copies(j) + [y2_copy(j), far_copy(j)]:
            copy.wait_send()

    loop(0, CHUNKS, sent)
    loop(1, CHIPS, lambda k: h_copy(k).wait_send())
    h_sib(c).wait_send()
    loop(1, SLOTS, lambda k: part_copy(k).wait_send())
    loop(1, PEERS, lambda k: peer_copy(*attention, k).wait_send())
    loop(1, PEERS, lambda k: peer_copy(*project, k).wait_send())


def place_kernel(map_ref, gat, part, out_hbm, part_out, sem, part_sem):
    last = pltpu.make_async_copy(part, part_out, part_sem)
    last.start()
    copies = []
    for group in range(SLOTS):
        for layer in range(LAYERS):
            copy = pltpu.make_async_copy(
                gat.at[map_ref[group], layer],
                out_hbm.at[layer, :, pl.ds(group * HD, HD)],
                sem.at[group, layer],
            )
            copy.start()
            copies.append(copy)
    for copy in copies:
        copy.wait()
    last.wait()


def on_device(
    hidden, resident, delta_codes, scales, owner_map, key_value_bias, queries, key_cache,
    value_cache, lengths,
):
    inverse = (ROPE_BASE ** (-2.0 * np.arange(HD // 2) / HD)).astype(np.float32)
    inverse = jnp.asarray(np.concatenate([inverse, inverse])[None, :])
    smem = pl.BlockSpec(memory_space=pltpu.SMEM)
    vmem = pl.BlockSpec(memory_space=pltpu.VMEM)
    hbm = pl.BlockSpec(memory_space=pltpu.HBM)
    anywhere = pl.BlockSpec(memory_space=pl.ANY)
    dma = pltpu.SemaphoreType.DMA
    f32, bf16 = jnp.float32, jnp.bfloat16
    part_shape = (LAYERS, 1, STEPS, HEADS // PEERS, HD)
    arrays = (
        owner_map, lengths, hidden, resident, delta_codes,
        scales.reshape(LAYERS, ROWS), key_value_bias, inverse,
        queries.reshape(LAYERS, QROWS, HD),
        key_cache.reshape(LAYERS, COLS, HD), value_cache.reshape(LAYERS, COLS, HD),
    )
    gathered, part, chosen = pl.pallas_call(
        gather_kernel,
        out_shape=(
            pltpu.VMEM((SLOTS, LAYERS, ROWS, HD), bf16),
            jax.ShapeDtypeStruct(part_shape, bf16),
            pltpu.SMEM((SLOTS,), jnp.int32),
        ),
        in_specs=[hbm, smem] + [hbm] * 9,
        out_specs=(vmem, vmem, smem),
        scratch_shapes=[
            pltpu.SMEM((SLOTS,), jnp.int32),
            pltpu.VMEM((LAYERS, 1, STEPS, ROWS), bf16),
            pltpu.VMEM((LAYERS, ROWS, SLOTS * HD), bf16),
            pltpu.VMEM((LAYERS, ROWS, HD), bf16),
            pltpu.VMEM((LAYERS, ROWS), bf16),
            pltpu.VMEM((LAYERS, SLOTS * HD), bf16),
            pltpu.VMEM((1, HD), f32),
            pltpu.VMEM((LAYERS, QROWS, HD), bf16),
            pltpu.VMEM((LAYERS, COLS, HD), bf16),
            pltpu.VMEM((LAYERS, COLS, HD), bf16),
            pltpu.VMEM((2, CHIPS, 16, 256), bf16),
            pltpu.VMEM((LAYERS, QROWS, HD), bf16),
            pltpu.VMEM((QROWS, COLS), f32),
            pltpu.VMEM((QROWS, HD), f32),
            pltpu.VMEM((QROWS, HD), f32),
            pltpu.VMEM((QROWS, HD), f32),
            pltpu.VMEM((QROWS, HD), f32),
            pltpu.VMEM((QROWS, HD), f32),
            pltpu.VMEM((PEERS, 3 * OWN, HD), bf16),
            pltpu.VMEM((PEERS, 3 * OWN, HD), bf16),
            pltpu.VMEM((SLOTS, LAYERS * STEPS, HD), f32),
            pltpu.VMEM((SLOTS, LAYERS * STEPS, HD), f32),
            pltpu.VMEM((PEERS // 2, 16, HD), f32),
            pltpu.VMEM((PEERS, 16, HD), f32),
            dma((10,)),
            dma((SLOTS, CHUNKS)),
            dma((SLOTS, LAYERS)),
            dma((3, CHUNKS)),
            dma((CHUNKS,)),
            dma((2, CHUNKS)),
            dma((CHUNKS,)),
            dma((8, LAYERS)),
            dma((CHIPS + 1,)),
            dma((CHIPS,)),
            pltpu.SemaphoreType.REGULAR,
            dma((PEERS,)),
            dma((PEERS,)),
            dma((SLOTS,)),
            dma((SLOTS,)),
            dma((PEERS,)),
            dma((PEERS,)),
        ],
        compiler_params=pltpu.CompilerParams(
            collective_id=0, has_side_effects=True, vmem_limit_bytes=40 * MIB
        ),
    )(*(a if a.size == 1 else pltpu.with_memory_space_constraint(a, pltpu.HBM) for a in arrays))
    return pl.pallas_call(
        place_kernel,
        out_shape=(
            jax.ShapeDtypeStruct((LAYERS, ROWS, SLOTS * HD), bf16),
            jax.ShapeDtypeStruct(part_shape, bf16),
        ),
        in_specs=[smem, vmem, vmem],
        out_specs=(anywhere, anywhere),
        scratch_shapes=[dma((SLOTS, LAYERS)), dma(())],
        compiler_params=pltpu.CompilerParams(vmem_limit_bytes=16 * MIB),
    )(chosen, gathered, part)


def solution(mesh):
    in_specs = (
        P(None, "replica", None, "tensor"),
        P(None, "tensor", None),
        P(None, "tensor", "replica"),
        P(None, "tensor", "replica"),
        P(),
        P(),
        P(None, "replica", None, None, None),
        P(None, "replica", "tensor", None, None),
        P(None, "replica", "tensor", None, None),
        P("replica"),
    )
    out_specs = (P(None, "tensor", None), P(None, "replica", None, "tensor", None))
    return jax.shard_map(
        on_device, mesh=mesh, in_specs=in_specs, out_specs=out_specs, check_vma=False
    )
```

time: 46.3 us -> 39.7 us (0.86)
  the two profiles are of different devices: /device:TPU:1 before, /device:TPU:2 now
where the time goes in v2:
time: 39.7 us; the launch traced here: 39.6 us
  Pallas kernels  38.3 us (96%)
  between operations  1.29 us (3%)
    pallas_call x1, Pallas kernels, on_device(): pl.pallas_call(gather_kernel, out_shape=(pltpu.VMEM((SLOTS, LAYERS, ROWS,...  36 us
    pallas_call x1, Pallas kernels, on_device(): pl.pallas_call(place_kernel, out_shape=(jax.ShapeDtypeStruct((LAYERS, ROW...  2.29 us

profile of v2, /device:TPU:2, one launch (start us, length us, event | category | flops | bytes accessed | tf_op | source)
XLA Modules:
  0.0 39.6 jit_solution(14581050966393052380)
XLA Ops:
  1.3 36.0 %shard_map.122 = (bf16[16,2,512,128]{3,2,1,0:T(8,128)(2,1)S(1)}, bf16[2,1,4,4,128]{4,3,2,1,0:T(4,128)(2,1)S(1)}, s32[16]{0:T(128)S(4)}) custom-call(s32[16]{0:T(128)} %map_hbm.1, s32[1]{0:T(128)S(6)} %copy.13.len_ref, bf16[2,1,4,512]{3,2,1,0:T(4,128)(2,1)} %hid_hbm.1, bf16[2,512,2048]{2,1,0:T(8,128)(2,1)} %res_hbm.1, bf16[2,512,128]{2,1,0:T(8,128)(2,1)} %code_hbm.1, ...), custom_call_target="tpu_custom_call" | custom-call | tf_op jit(solution)/shard_map/pallas_call | solution.py:487
  37.3 2.3 %shard_map.123 = (bf16[2,512,2048]{2,1,0:T(8,128)(2,1)}, bf16[2,1,4,4,128]{4,3,2,1,0:T(4,128)(2,1)}) custom-call(s32[16]{0:T(128)S(4)} %get-tuple-element.5.map_ref, bf16[16,2,512,128]{3,2,1,0:T(8,128)(2,1)S(1)} %get-tuple-element.6.gat, bf16[2,1,4,4,128]{4,3,2,1,0:T(4,128)(2,1)S(1)} %get-tuple-element.7.part), custom_call_target="tpu_custom_call" | custom-call | tf_op jit(solution)/shard_map/pallas_call | solution.py:543

commit v3 on v2

--- a/solution.py
+++ b/solution.py
@@ -20,6 +20,7 @@
 HD = 128
 SLOTS = 16
 PEERS = 16
+RANKS = 8
 HEADS = 64
 KVH = 8
 QROWS = STEPS * HEADS
@@ -46,20 +47,26 @@
     map_hbm, len_ref, hid_hbm, res_hbm, code_hbm, scale_hbm, bias_hbm, inv_hbm, q_hbm, k_hbm, v_hbm,
     gat, out_ref, map_out,
     map_ref, hid_ref, res, code_ref, scale_ref, bias_ref, inv_ref, q_ref, kbuf, vbuf,
-    hall, qp, sbuf, top, peak, total, acc, side, asend, arecv, part, proj, psend, precv,
+    hall, qp, sbuf, top, peak, total, acc, side, asend, arecv, part, proj, psend, precv, pair_own, pair_in,
     load_sem, r_sem, sib_r_sem, own_sem, y2_sem, cross_sem, far_sem, sib_sem,
-    h_r_sem, h_sem, token_sem, as_sem, ar_sem, part_sem, part_r_sem, ps_sem, pr_sem,
+    h_r_sem, h_sem, token_sem, as_sem, ar_sem, part_sem, part_r_sem, ps_sem, pr_sem, pair_sem,
 ):
     xh, y, c, t = place()
     me = slot_of(xh, y, c)
 
     pairs = [
-        (map_hbm, map_ref), (scale_hbm, scale_ref), (code_hbm, code_ref), (res_hbm, res),
-        (hid_hbm, hid_ref), (q_hbm, q_ref), (k_hbm, kbuf), (v_hbm, vbuf),
-        (bias_hbm, bias_ref), (inv_hbm, inv_ref),
+        (map_hbm, map_ref), (hid_hbm, hid_ref), (scale_hbm, scale_ref), (code_hbm, code_ref),
+    ]
+    for j in range(CHUNKS):
+        rows = pl.ds((j % 2) * HALF, HALF)
+        pairs.append((res_hbm.at[j // 2, rows, :], res.at[j // 2, rows, :]))
+    pairs += [
+        (q_hbm, q_ref), (k_hbm, kbuf), (v_hbm, vbuf), (bias_hbm, bias_ref), (inv_hbm, inv_ref),
     ]
     loads = [pltpu.make_async_copy(a, b, load_sem.at[i]) for i, (a, b) in enumerate(pairs)]
-    for load in loads:
+    load_map, load_hid, load_scale, load_code = loads[:4]
+    load_res, (load_q, load_k, load_v, load_bias, load_inv) = loads[4:8], loads[8:]
+    for load in loads[:8]:
         load.start()
 
     def loop(low, high, body):
@@ -88,22 +95,35 @@
 
     loop(1, CHIPS, greet_chip)
 
+    z, xl = t // 2, t % 2
+    low, high_rank = z < RANKS // 2, z >= RANKS // 2
+
+    def rank_device(k):
+        return (me, k * 2 + xl)
+
+    to_pair = (me, z * 2 + 1 - xl)
+
     def greet(k):
-        pl.semaphore_signal(barrier, inc=1, device_id=(me, k), device_id_type=MESH)
-
-    loop(t + 1, PEERS, greet)
-
-    loads[0].wait()
+        pl.semaphore_signal(barrier, inc=1, device_id=rank_device(k), device_id_type=MESH)
+
+    loop(z + 1, RANKS, greet)
+
+    @pl.when(xl == 0)
+    def _():
+        pl.semaphore_signal(barrier, inc=1, device_id=to_pair, device_id_type=MESH)
+
+    load_map.wait()
     group = jnp.int32(0)
     for g in range(SLOTS):
         group = group + jnp.where(map_ref[g] == me, g, 0)
         map_out[g] = map_ref[g]
-    for load in loads[1:5]:
-        load.wait()
     group_all = jnp.broadcast_to(group.astype(jnp.float32), (HD, HD)).astype(jnp.bfloat16)
-    for layer in range(LAYERS):
-        for p in range(ROWS // HD):
-            rows = pl.ds(p * HD, HD)
+
+    def own_block(j):
+        load_res[j].wait()
+        layer = j // 2
+        for p in range(HALF // HD):
+            rows = pl.ds((j % 2) * HALF + p * HD, HD)
             line = scale_ref[pl.ds(layer, 1), rows].astype(jnp.float32)
             column = jnp.transpose(jnp.broadcast_to(line, (HD, HD)))
             code = code_ref[layer, rows, :].astype(jnp.float32)
@@ -112,6 +132,8 @@
                 base = jnp.where(group_all == g, res[layer, rows, g * HD : (g + 1) * HD], base)
             base = base.astype(jnp.float32)
             gat[me, layer, rows, :] = (base + code * column).astype(jnp.bfloat16)
+
+    load_hid.wait()
     halves = [
         hid_ref[layer, 0, :, h * 256 : (h + 1) * 256].astype(jnp.float32)
         for h in range(2)
@@ -119,7 +141,14 @@
     ]
     hall[c, chip] = jnp.concatenate(halves, axis=0).astype(jnp.bfloat16)
 
-    pl.semaphore_wait(barrier, CHIPS + t)
+    load_scale.wait()
+    load_code.wait()
+    own_block(0)
+    own_block(1)
+    for load in loads[8:]:
+        load.start()
+
+    pl.semaphore_wait(barrier, CHIPS + z + xl)
 
     def copy_of(src, dst, s_sem, rr_sem, target):
         return pltpu.make_async_remote_copy(
@@ -204,14 +233,22 @@
         for copy in own_copies(j):
             copy.start()
 
-    loop(0, CHUNKS - 1, own_step)
+    loop(0, 2, own_step)
+    own_block(2)
+    own_step(2)
+    own_block(3)
+    pl.when(low)(functools.partial(own_step, 3))
 
     def answer(k):
-        pl.semaphore_signal(token_sem, inc=1, device_id=(me, k), device_id_type=MESH)
-
-    loop(0, t, answer)
-
-    loads[5].wait()
+        pl.semaphore_signal(token_sem, inc=1, device_id=rank_device(k), device_id_type=MESH)
+
+    loop(0, z, answer)
+
+    @pl.when(xl == 1)
+    def _():
+        pl.semaphore_signal(token_sem, inc=1, device_id=to_pair, device_id_type=MESH)
+
+    load_q.wait()
     row = lax.broadcasted_iota(jnp.int32, (QROWS, QROWS), 0)
     col = lax.broadcasted_iota(jnp.int32, (QROWS, QROWS), 1)
     source = ((row // STEPS) % STEPS) * HEADS + (row // OWN) * STEPS + row % STEPS
@@ -262,8 +299,8 @@
                 preferred_element_type=jnp.float32,
             )
         whole = jnp.broadcast_to(jnp.sum(total[...], axis=1, keepdims=True), (QROWS, HD))
-        asend[:, layer * OWN : (layer + 1) * OWN, :] = (
-            (acc[...] / whole).astype(jnp.bfloat16).reshape(PEERS, OWN, HD)
+        asend[:, layer * 2 * OWN : (layer + 1) * 2 * OWN, :] = (
+            (acc[...] / whole).astype(jnp.bfloat16).reshape(RANKS, 2 * OWN, HD)
         )
         rest = peak[...] * EXP_SCALE + jnp.log(whole) * math.log2(math.e)
         kept = side[...] if layer else jnp.zeros((QROWS, HD), jnp.float32)
@@ -273,17 +310,52 @@
             kept = jnp.where(lane == 3 * layer + i, term, kept)
         side[...] = kept
 
-    loads[6].wait()
+    def rank_copy(src, dst, s_sem, rr_sem, k):
+        target = (z + k) % RANKS
+        return copy_of(
+            src(target), dst(z), s_sem.at[target], rr_sem.at[z], rank_device(target)
+        )
+
+    def rank_arrived(src, dst, s_sem, rr_sem, k):
+        other = (z + k) % RANKS
+        copy_of(
+            src(other), dst(other), s_sem.at[other], rr_sem.at[other], rank_device(other)
+        ).wait_recv()
+
+    def run_of(ref, layer):
+        return lambda rank: ref.at[rank, 0:32] if layer == 0 else ref.at[rank, 32:80]
+
+    attention = [
+        (run_of(asend, layer), run_of(arecv, layer), as_sem.at[layer], ar_sem.at[layer])
+        for layer in range(LAYERS)
+    ]
+    project = (lambda rank: psend.at[rank], lambda rank: precv.at[rank], ps_sem, pr_sem)
+
+    def answered():
+        answers = (RANKS - 1 - z) + (1 - xl)
+        pl.when(answers > 0)(lambda: pl.semaphore_wait(token_sem, answers))
+
+    def send_attention(layer):
+        loop(1, RANKS, lambda k: rank_copy(*attention[layer], k).start())
+
+    def send_project():
+        loop(1, RANKS, lambda k: rank_copy(*project, k).start())
+
+    load_k.wait()
     scores(0)
-    loads[7].wait()
-    values(0)
-    own_step(CHUNKS - 1)
-    for layer in range(LAYERS):
-        sib_send(0, layer)
     loop(1, CHIPS, h_arrived)
     h_sib(c).start()
-    scores(1)
-    loop(0, 2, y2_step)
+    load_v.wait()
+    values(0)
+
+    @pl.when(high_rank)
+    def _():
+        answered()
+        send_attention(0)
+
+    for layer in range(LAYERS):
+        sib_send(0, layer)
+    pl.when(low)(lambda: loop(0, 2, y2_step))
     h_sib(1 - c).wait_recv()
 
     rows8 = lax.broadcasted_iota(jnp.int32, (SLOTS, LAYERS * STEPS, HD), 1)
@@ -315,23 +387,22 @@
     loop(1, SLOTS, lambda k: part_copy(k).start())
     proj[me] = part[c * CHIPS + chip]
 
+    @pl.when(high_rank)
+    def _():
+        own_step(3)
+        loop(0, 2, y2_step)
+
+    scores(1)
     values(1)
-    asend[:, 2 * OWN :, :] = side[...].astype(jnp.bfloat16).reshape(PEERS, OWN, HD)
+    notes = side[...].reshape(RANKS, 2 * OWN, HD)
+    second = pltpu.roll(notes[:, OWN:].reshape(RANKS * OWN, HD), HD // 2, 1)
+    lane3 = lax.broadcasted_iota(jnp.int32, (RANKS, OWN, HD), 2)
+    notes = jnp.where(lane3 < HD // 2, notes[:, :OWN], second.reshape(RANKS, OWN, HD))
+    asend[:, 4 * OWN :, :] = notes.astype(jnp.bfloat16)
+    pl.when(high_rank)(lambda: send_attention(1))
     loop(2, CHUNKS, y2_step)
-    loop(0, 2, cross_step)
-
-    def peer_copy(src, dst, s_sem, rr_sem, k):
-        target = (t + k) % PEERS
-        return copy_of(src(target), dst.at[t], s_sem.at[target], rr_sem.at[t], (me, target))
-
-    def peer_arrived(src, dst, s_sem, rr_sem, k):
-        other = (t + k) % PEERS
-        copy_of(
-            src(other), dst.at[other], s_sem.at[other], rr_sem.at[other], (me, other)
-        ).wait_recv()
-
-    attention = (lambda target: asend.at[target], arecv, as_sem, ar_sem)
-    project = (lambda target: psend.at[target // 2], precv, ps_sem, pr_sem)
+    loop(0, CHUNKS, cross_step)
+
     loop(1, SLOTS, part_arrived)
     for g in range(SLOTS):
         slot_all = jnp.broadcast_to(map_ref[g], (LAYERS * STEPS, HD))
@@ -339,16 +410,10 @@
         for slot in range(1, SLOTS):
             line = jnp.where(slot_all == slot, proj[slot], line)
         psend[g // 2, (g % 2) * 8 : (g % 2) * 8 + 8, :] = line
-    precv[t] = psend[t // 2]
-    arecv[t] = asend[t]
-
-    def send_peers():
-        pl.when(t < PEERS - 1)(lambda: pl.semaphore_wait(token_sem, PEERS - 1 - t))
-        loop(1, PEERS, lambda k: peer_copy(*project, k).start())
-        loop(1, PEERS, lambda k: peer_copy(*attention, k).start())
-
-    pl.when(t >= PEERS // 2)(send_peers)
-    loop(2, CHUNKS, cross_step)
+    precv[z] = psend[z]
+    arecv[z] = asend[z]
+
+    pl.when(high_rank)(send_project)
 
     def opposite_step(j):
         arrived(slot_of(xh, (y + 4 + 1 - 2 * (j % 2)) % 4, c), j)
@@ -358,14 +423,21 @@
         far_copy(j).start()
 
     loop(0, CHUNKS, far_step)
-    pl.when(t < PEERS // 2)(send_peers)
+
+    @pl.when(low)
+    def _():
+        answered()
+        send_project()
+        send_attention(0)
+        send_attention(1)
+
     loop(0, CHUNKS, opposite_step)
     for layer in range(LAYERS):
         for i in range(4):
             sib_send(i + 1, layer)
 
-    for load in loads[8:]:
-        load.wait()
+    load_bias.wait()
+    load_inv.wait()
     turn_row = lax.broadcasted_iota(jnp.int32, (LAYERS * STEPS, HD), 0)
     turn_lane = lax.broadcasted_iota(jnp.int32, (LAYERS * STEPS, HD), 1)
     angle = (length + turn_row % STEPS).astype(jnp.float32) * inv_ref[...]
@@ -374,30 +446,62 @@
     head = t // 2
     bias = bias_ref[:, pl.ds(pl.multiple_of(head * 2 * HD, 2 * HD), 2 * HD)].astype(jnp.float32)
 
-    for layer in range(LAYERS):
-        for i, slot in ((5, x_up), (6, x_down), (7, x_far)):
-            loop(2 * layer, 2 * layer + 2, lambda j, slot=slot: arrived(slot, j))
-            sib_send(i, layer)
-
-    loop(1, PEERS, lambda k: peer_arrived(*attention, k))
-    joined = []
-    sides = [arecv[p, 2 * OWN :, :].astype(jnp.float32) for p in range(PEERS)]
-    for layer in range(LAYERS):
-        logs = [sum(x[:, 3 * layer + i : 3 * layer + i + 1] for i in range(3)) for x in sides]
+    def last_pieces():
+        for layer in range(LAYERS):
+            for i, slot in ((5, x_up), (6, x_down), (7, x_far)):
+                loop(2 * layer, 2 * layer + 2, lambda j, slot=slot: arrived(slot, j))
+                sib_send(i, layer)
+
+    pl.when(low)(last_pieces)
+
+    for layer in range(LAYERS):
+        loop(1, RANKS, lambda k, layer=layer: rank_arrived(*attention[layer], k))
+    lane32 = lax.broadcasted_iota(jnp.int32, (2 * OWN, HD), 1)
+    sides = [arecv[p, 4 * OWN :, :].astype(jnp.float32) for p in range(RANKS)]
+    notes = jnp.zeros((2 * OWN, HD), jnp.float32)
+    for layer in range(LAYERS):
+        logs = []
+        for x in sides:
+            firsts = (3 * layer, 3 * layer + HD // 2)
+            columns = [sum(x[:, n + i : n + i + 1] for i in range(3)) for n in firsts]
+            logs.append(jnp.concatenate(columns, axis=0))
         high = functools.reduce(jnp.maximum, logs)
-        whole = jnp.zeros((OWN, 1), jnp.float32)
-        summed = jnp.zeros((OWN, HD), jnp.float32)
-        for p in range(PEERS):
+        whole = jnp.zeros((2 * OWN, 1), jnp.float32)
+        summed = jnp.zeros((2 * OWN, HD), jnp.float32)
+        rows = slice(layer * 2 * OWN, (layer + 1) * 2 * OWN)
+        for p in range(RANKS):
             factor = jnp.exp2(logs[p] - high)
             whole = whole + factor
-            summed = summed + factor * arecv[p, layer * OWN : (layer + 1) * OWN, :].astype(jnp.float32)
+            summed = summed + factor * arecv[p, rows, :].astype(jnp.float32)
+        for o in range(2):
+            pair_own[o, layer * OWN : (layer + 1) * OWN, :] = summed[o * OWN : (o + 1) * OWN]
+        notes = jnp.where(lane32 == 2 * layer, high, notes)
+        notes = jnp.where(lane32 == 2 * layer + 1, whole, notes)
+    loop(1, RANKS, lambda k: rank_arrived(*project, k))
+    projected = precv[0]
+    for p in range(1, RANKS):
+        projected = projected + precv[p]
+    for o in range(2):
+        pair_own[o, 2 * OWN : 3 * OWN, :] = notes[o * OWN : (o + 1) * OWN]
+        pair_own[o, 3 * OWN :, :] = projected
+
+    pair = copy_of(pair_own.at[1 - xl], pair_in, pair_sem.at[0], pair_sem.at[1], to_pair)
+    pair.start()
+    pl.when(high_rank)(last_pieces)
+    pair.wait_recv()
+    joined = []
+    for layer in range(LAYERS):
+        sums, highs, wholes = [], [], []
+        for half in (pair_own.at[xl], pair_in):
+            sums.append(half[layer * OWN : (layer + 1) * OWN, :])
+            highs.append(half[2 * OWN : 3 * OWN, 2 * layer : 2 * layer + 1])
+            wholes.append(half[2 * OWN : 3 * OWN, 2 * layer + 1 : 2 * layer + 2])
+        high = jnp.maximum(*highs)
+        factors = [jnp.exp2(h - high) for h in highs]
+        whole = wholes[0] * factors[0] + wholes[1] * factors[1]
+        summed = sums[0] * factors[0] + sums[1] * factors[1]
         joined.append((high, whole, summed))
-
-    loop(1, PEERS, lambda k: peer_arrived(*project, k))
-    projected = precv[0]
-    for p in range(1, PEERS):
-        projected = projected + precv[p]
-    projected = projected * (ROWS * PEERS) ** -0.5
+    projected = (pair_own[xl, 3 * OWN :, :] + pair_in[3 * OWN :, :]) * (ROWS * PEERS) ** -0.5
 
     def biased(kind):
         lines = [
@@ -443,8 +547,10 @@
     loop(1, CHIPS, lambda k: h_copy(k).wait_send())
     h_sib(c).wait_send()
     loop(1, SLOTS, lambda k: part_copy(k).wait_send())
-    loop(1, PEERS, lambda k: peer_copy(*attention, k).wait_send())
-    loop(1, PEERS, lambda k: peer_copy(*project, k).wait_send())
+    for layer in range(LAYERS):
+        loop(1, RANKS, lambda k, layer=layer: rank_copy(*attention[layer], k).wait_send())
+    loop(1, RANKS, lambda k: rank_copy(*project, k).wait_send())
+    pair.wait_send()
 
 
 def place_kernel(map_ref, gat, part, out_hbm, part_out, sem, part_sem):
@@ -512,13 +618,15 @@
             pltpu.VMEM((QROWS, HD), f32),
             pltpu.VMEM((QROWS, HD), f32),
             pltpu.VMEM((QROWS, HD), f32),
-            pltpu.VMEM((PEERS, 3 * OWN, HD), bf16),
-            pltpu.VMEM((PEERS, 3 * OWN, HD), bf16),
+            pltpu.VMEM((RANKS, 5 * OWN, HD), bf16),
+            pltpu.VMEM((RANKS, 5 * OWN, HD), bf16),
             pltpu.VMEM((SLOTS, LAYERS * STEPS, HD), f32),
             pltpu.VMEM((SLOTS, LAYERS * STEPS, HD), f32),
-            pltpu.VMEM((PEERS // 2, 16, HD), f32),
-            pltpu.VMEM((PEERS, 16, HD), f32),
-            dma((10,)),
+            pltpu.VMEM((RANKS, 16, HD), f32),
+            pltpu.VMEM((RANKS, 16, HD), f32),
+            pltpu.VMEM((2, 4 * OWN, HD), f32),
+            pltpu.VMEM((4 * OWN, HD), f32),
+            dma((13,)),
             dma((SLOTS, CHUNKS)),
             dma((SLOTS, LAYERS)),
             dma((3, CHUNKS)),
@@ -529,12 +637,13 @@
             dma((CHIPS + 1,)),
             dma((CHIPS,)),
             pltpu.SemaphoreType.REGULAR,
-            dma((PEERS,)),
-            dma((PEERS,)),
+            dma((LAYERS, RANKS)),
+            dma((LAYERS, RANKS)),
             dma((SLOTS,)),
             dma((SLOTS,)),
-            dma((PEERS,)),
-            dma((PEERS,)),
+            dma((RANKS,)),
+            dma((RANKS,)),
+            dma((2,)),
         ],
         compiler_params=pltpu.CompilerParams(
             collective_id=0, has_side_effects=True, vmem_limit_bytes=40 * MIB

time: 39.7 us -> 36.9 us (0.929)
  Pallas kernels: 38.3 us -> 35.5 us
    pallas_call x1, Pallas kernels: 36 us -> 33.2 us  [on_device(): pl.pallas_call(gather_kernel, out_shape=(pltpu.VMEM((SLOTS, LAYERS, ROWS,...]
where the time goes in v3:
time: 36.9 us; the launch traced here: 36.8 us
  Pallas kernels  35.5 us (96%)
  between operations  1.29 us (3%)
    pallas_call x1, Pallas kernels, on_device(): pl.pallas_call(gather_kernel, out_shape=(pltpu.VMEM((SLOTS, LAYERS, ROWS,...  33.2 us
    pallas_call x1, Pallas kernels, on_device(): pl.pallas_call(place_kernel, out_shape=(jax.ShapeDtypeStruct((LAYERS, ROW...  2.29 us

profile of v3, /device:TPU:2, one launch (start us, length us, event | category | flops | bytes accessed | tf_op | source)
XLA Modules:
  0.0 36.8 jit_solution(6462633689723842119)
XLA Ops:
  1.3 33.2 %shard_map.122 = (bf16[16,2,512,128]{3,2,1,0:T(8,128)(2,1)S(1)}, bf16[2,1,4,4,128]{4,3,2,1,0:T(4,128)(2,1)S(1)}, s32[16]{0:T(128)S(4)}) custom-call(s32[16]{0:T(128)} %map_hbm.1, s32[1]{0:T(128)S(6)} %copy.13.len_ref, bf16[2,1,4,512]{3,2,1,0:T(4,128)(2,1)} %hid_hbm.1, bf16[2,512,2048]{2,1,0:T(8,128)(2,1)} %res_hbm.1, bf16[2,512,128]{2,1,0:T(8,128)(2,1)} %code_hbm.1, ...), custom_call_target="tpu_custom_call" | custom-call | tf_op jit(solution)/shard_map/pallas_call | solution.py:593
  34.5 2.3 %shard_map.123 = (bf16[2,512,2048]{2,1,0:T(8,128)(2,1)}, bf16[2,1,4,4,128]{4,3,2,1,0:T(4,128)(2,1)}) custom-call(s32[16]{0:T(128)S(4)} %get-tuple-element.5.map_ref, bf16[16,2,512,128]{3,2,1,0:T(8,128)(2,1)S(1)} %get-tuple-element.6.gat, bf16[2,1,4,4,128]{4,3,2,1,0:T(4,128)(2,1)S(1)} %get-tuple-element.7.part), custom_call_target="tpu_custom_call" | custom-call | tf_op jit(solution)/shard_map/pallas_call | solution.py:652

commit v4 on v3

--- a/solution.py
+++ b/solution.py
@@ -141,13 +141,6 @@
     ]
     hall[c, chip] = jnp.concatenate(halves, axis=0).astype(jnp.bfloat16)
 
-    load_scale.wait()
-    load_code.wait()
-    own_block(0)
-    own_block(1)
-    for load in loads[8:]:
-        load.start()
-
     pl.semaphore_wait(barrier, CHIPS + z + xl)
 
     def copy_of(src, dst, s_sem, rr_sem, target):
@@ -227,17 +220,24 @@
         for copy in cross_copies(j):
             copy.start()
 
+    def far_step(j):
+        arrived(s_far, j)
+        far_copy(j).start()
+
     loop(1, CHIPS, lambda k: h_copy(k).start())
 
     def own_step(j):
         for copy in own_copies(j):
             copy.start()
 
-    loop(0, 2, own_step)
-    own_block(2)
-    own_step(2)
-    own_block(3)
-    pl.when(low)(functools.partial(own_step, 3))
+    load_scale.wait()
+    load_code.wait()
+    for j in range(CHUNKS):
+        own_block(j)
+        own_step(j)
+        if j == 0:
+            for load in loads[8:]:
+                load.start()
 
     def answer(k):
         pl.semaphore_signal(token_sem, inc=1, device_id=rank_device(k), device_id_type=MESH)
@@ -387,21 +387,44 @@
     loop(1, SLOTS, lambda k: part_copy(k).start())
     proj[me] = part[c * CHIPS + chip]
 
-    @pl.when(high_rank)
+    scores(1)
+    @pl.when(low)
     def _():
-        own_step(3)
-        loop(0, 2, y2_step)
-
-    scores(1)
+        loop(2, CHUNKS, y2_step)
+        loop(0, 2, cross_step)
+
+    pl.when(high_rank)(lambda: loop(0, 2, y2_step))
     values(1)
     notes = side[...].reshape(RANKS, 2 * OWN, HD)
     second = pltpu.roll(notes[:, OWN:].reshape(RANKS * OWN, HD), HD // 2, 1)
     lane3 = lax.broadcasted_iota(jnp.int32, (RANKS, OWN, HD), 2)
     notes = jnp.where(lane3 < HD // 2, notes[:, :OWN], second.reshape(RANKS, OWN, HD))
     asend[:, 4 * OWN :, :] = notes.astype(jnp.bfloat16)
-    pl.when(high_rank)(lambda: send_attention(1))
-    loop(2, CHUNKS, y2_step)
-    loop(0, CHUNKS, cross_step)
+    @pl.when(high_rank)
+    def _():
+        send_attention(1)
+        loop(2, CHUNKS, y2_step)
+        loop(0, 2, cross_step)
+
+
+    def opposite_step(j):
+        arrived(slot_of(xh, (y + 4 + 1 - 2 * (j % 2)) % 4, c), j)
+
+    def far_steps():
+        loop(2, CHUNKS, far_step)
+        loop(0, CHUNKS, opposite_step)
+        for layer in range(LAYERS):
+            for i in range(4):
+                sib_send(i + 1, layer)
+
+    @pl.when(low)
+    def _():
+        loop(2, CHUNKS, cross_step)
+        loop(0, 2, far_step)
+        far_steps()
+        answered()
+        send_attention(0)
+        send_attention(1)
 
     loop(1, SLOTS, part_arrived)
     for g in range(SLOTS):
@@ -413,28 +436,13 @@
     precv[z] = psend[z]
     arecv[z] = asend[z]
 
-    pl.when(high_rank)(send_project)
-
-    def opposite_step(j):
-        arrived(slot_of(xh, (y + 4 + 1 - 2 * (j % 2)) % 4, c), j)
-
-    def far_step(j):
-        arrived(s_far, j)
-        far_copy(j).start()
-
-    loop(0, CHUNKS, far_step)
-
-    @pl.when(low)
+    send_project()
+
+    @pl.when(high_rank)
     def _():
-        answered()
-        send_project()
-        send_attention(0)
-        send_attention(1)
-
-    loop(0, CHUNKS, opposite_step)
-    for layer in range(LAYERS):
-        for i in range(4):
-            sib_send(i + 1, layer)
+        loop(2, CHUNKS, cross_step)
+        loop(0, 2, far_step)
+        far_steps()
 
     load_bias.wait()
     load_inv.wait()
@@ -446,13 +454,13 @@
     head = t // 2
     bias = bias_ref[:, pl.ds(pl.multiple_of(head * 2 * HD, 2 * HD), 2 * HD)].astype(jnp.float32)
 
-    def last_pieces():
-        for layer in range(LAYERS):
-            for i, slot in ((5, x_up), (6, x_down), (7, x_far)):
-                loop(2 * layer, 2 * layer + 2, lambda j, slot=slot: arrived(slot, j))
-                sib_send(i, layer)
-
-    pl.when(low)(last_pieces)
+    def last_pieces(layer):
+        for i, slot in ((5, x_up), (6, x_down), (7, x_far)):
+            loop(2 * layer, 2 * layer + 2, lambda j, slot=slot: arrived(slot, j))
+            sib_send(i, layer)
+
+    last_pieces(0)
+    pl.when(z < 2)(lambda: last_pieces(1))
 
     for layer in range(LAYERS):
         loop(1, RANKS, lambda k, layer=layer: rank_arrived(*attention[layer], k))
@@ -477,18 +485,27 @@
             pair_own[o, layer * OWN : (layer + 1) * OWN, :] = summed[o * OWN : (o + 1) * OWN]
         notes = jnp.where(lane32 == 2 * layer, high, notes)
         notes = jnp.where(lane32 == 2 * layer + 1, whole, notes)
+    for o in range(2):
+        pair_own[o, 2 * OWN : 3 * OWN, :] = notes[o * OWN : (o + 1) * OWN]
+
+    def pair_copy(n, low_row, count):
+        rows = pl.ds(low_row, count)
+        return copy_of(
+            pair_own.at[1 - xl, rows, :], pair_in.at[rows, :],
+            pair_sem.at[n, 0], pair_sem.at[n, 1], to_pair,
+        )
+
+    pair = [pair_copy(0, 0, 3 * OWN), pair_copy(1, 3 * OWN, OWN)]
+    pair[0].start()
     loop(1, RANKS, lambda k: rank_arrived(*project, k))
     projected = precv[0]
     for p in range(1, RANKS):
         projected = projected + precv[p]
     for o in range(2):
-        pair_own[o, 2 * OWN : 3 * OWN, :] = notes[o * OWN : (o + 1) * OWN]
         pair_own[o, 3 * OWN :, :] = projected
-
-    pair = copy_of(pair_own.at[1 - xl], pair_in, pair_sem.at[0], pair_sem.at[1], to_pair)
-    pair.start()
-    pl.when(high_rank)(last_pieces)
-    pair.wait_recv()
+    pair[1].start()
+    pl.when(z >= 2)(lambda: last_pieces(1))
+    pair[0].wait_recv()
     joined = []
     for layer in range(LAYERS):
         sums, highs, wholes = [], [], []
@@ -501,6 +518,7 @@
         whole = wholes[0] * factors[0] + wholes[1] * factors[1]
         summed = sums[0] * factors[0] + sums[1] * factors[1]
         joined.append((high, whole, summed))
+    pair[1].wait_recv()
     projected = (pair_own[xl, 3 * OWN :, :] + pair_in[3 * OWN :, :]) * (ROWS * PEERS) ** -0.5
 
     def biased(kind):
@@ -550,7 +568,8 @@
     for layer in range(LAYERS):
         loop(1, RANKS, lambda k, layer=layer: rank_copy(*attention[layer], k).wait_send())
     loop(1, RANKS, lambda k: rank_copy(*project, k).wait_send())
-    pair.wait_send()
+    for copy in pair:
+        copy.wait_send()
 
 
 def place_kernel(map_ref, gat, part, out_hbm, part_out, sem, part_sem):
@@ -643,7 +662,7 @@
             dma((SLOTS,)),
             dma((RANKS,)),
             dma((RANKS,)),
-            dma((2,)),
+            dma((2, 2)),
         ],
         compiler_params=pltpu.CompilerParams(
             collective_id=0, has_side_effects=True, vmem_limit_bytes=40 * MIB

time: 36.9 us -> 35.6 us (0.965)
  Pallas kernels: 35.5 us -> 34.2 us
    pallas_call x1, Pallas kernels: 33.2 us -> 31.9 us  [on_device(): pl.pallas_call(gather_kernel, out_shape=(pltpu.VMEM((SLOTS, LAYERS, ROWS,...]
where the time goes in v4:
time: 35.6 us; the launch traced here: 35.5 us
  Pallas kernels  34.2 us (96%)
  between operations  1.29 us (4%)
    pallas_call x1, Pallas kernels, on_device(): pl.pallas_call(gather_kernel, out_shape=(pltpu.VMEM((SLOTS, LAYERS, ROWS,...  31.9 us
    pallas_call x1, Pallas kernels, on_device(): pl.pallas_call(place_kernel, out_shape=(jax.ShapeDtypeStruct((LAYERS, ROW...  2.29 us

profile of v4, /device:TPU:2, one launch (start us, length us, event | category | flops | bytes accessed | tf_op | source)
XLA Modules:
  0.0 35.5 jit_solution(13267054497114889434)
XLA Ops:
  1.3 31.9 %shard_map.122 = (bf16[16,2,512,128]{3,2,1,0:T(8,128)(2,1)S(1)}, bf16[2,1,4,4,128]{4,3,2,1,0:T(4,128)(2,1)S(1)}, s32[16]{0:T(128)S(4)}) custom-call(s32[16]{0:T(128)} %map_hbm.1, s32[1]{0:T(128)S(6)} %copy.13.len_ref, bf16[2,1,4,512]{3,2,1,0:T(4,128)(2,1)} %hid_hbm.1, bf16[2,512,2048]{2,1,0:T(8,128)(2,1)} %res_hbm.1, bf16[2,512,128]{2,1,0:T(8,128)(2,1)} %code_hbm.1, ...), custom_call_target="tpu_custom_call" | custom-call | tf_op jit(solution)/shard_map/pallas_call | solution.py:612
  33.2 2.3 %shard_map.123 = (bf16[2,512,2048]{2,1,0:T(8,128)(2,1)}, bf16[2,1,4,4,128]{4,3,2,1,0:T(4,128)(2,1)}) custom-call(s32[16]{0:T(128)S(4)} %get-tuple-element.5.map_ref, bf16[16,2,512,128]{3,2,1,0:T(8,128)(2,1)S(1)} %get-tuple-element.6.gat, bf16[2,1,4,4,128]{4,3,2,1,0:T(4,128)(2,1)S(1)} %get-tuple-element.7.part), custom_call_target="tpu_custom_call" | custom-call | tf_op jit(solution)/shard_map/pallas_call | solution.py:671

commit v5 on v4

--- a/solution.py
+++ b/solution.py
@@ -311,7 +311,7 @@
         side[...] = kept
 
     def rank_copy(src, dst, s_sem, rr_sem, k):
-        target = (z + k) % RANKS
+        target = k - 1 + (k - 1 - z + RANKS) // RANKS
         return copy_of(
             src(target), dst(z), s_sem.at[target], rr_sem.at[z], rank_device(target)
         )
@@ -460,7 +460,7 @@
             sib_send(i, layer)
 
     last_pieces(0)
-    pl.when(z < 2)(lambda: last_pieces(1))
+    pl.when(z < 3)(lambda: last_pieces(1))
 
     for layer in range(LAYERS):
         loop(1, RANKS, lambda k, layer=layer: rank_arrived(*attention[layer], k))
@@ -504,7 +504,7 @@
     for o in range(2):
         pair_own[o, 3 * OWN :, :] = projected
     pair[1].start()
-    pl.when(z >= 2)(lambda: last_pieces(1))
+    pl.when(z >= 3)(lambda: last_pieces(1))
     pair[0].wait_recv()
     joined = []
     for layer in range(LAYERS):

time: 35.6 us -> 35.4 us (level)
  no operation moved by 1% of the time
where the time goes in v5:
time: 35.4 us; the launch traced here: 35.3 us
  Pallas kernels  34 us (96%)
  between operations  1.29 us (4%)
    pallas_call x1, Pallas kernels, on_device(): pl.pallas_call(gather_kernel, out_shape=(pltpu.VMEM((SLOTS, LAYERS, ROWS,...  31.7 us
    pallas_call x1, Pallas kernels, on_device(): pl.pallas_call(place_kernel, out_shape=(jax.ShapeDtypeStruct((LAYERS, ROW...  2.29 us

profile of v5, /device:TPU:2, one launch (start us, length us, event | category | flops | bytes accessed | tf_op | source)
XLA Modules:
  0.0 35.3 jit_solution(5655227791234176823)
XLA Ops:
  1.3 31.7 %shard_map.122 = (bf16[16,2,512,128]{3,2,1,0:T(8,128)(2,1)S(1)}, bf16[2,1,4,4,128]{4,3,2,1,0:T(4,128)(2,1)S(1)}, s32[16]{0:T(128)S(4)}) custom-call(s32[16]{0:T(128)} %map_hbm.1, s32[1]{0:T(128)S(6)} %copy.13.len_ref, bf16[2,1,4,512]{3,2,1,0:T(4,128)(2,1)} %hid_hbm.1, bf16[2,512,2048]{2,1,0:T(8,128)(2,1)} %res_hbm.1, bf16[2,512,128]{2,1,0:T(8,128)(2,1)} %code_hbm.1, ...), custom_call_target="tpu_custom_call" | custom-call | tf_op jit(solution)/shard_map/pallas_call | solution.py:612
  33.0 2.3 %shard_map.123 = (bf16[2,512,2048]{2,1,0:T(8,128)(2,1)}, bf16[2,1,4,4,128]{4,3,2,1,0:T(4,128)(2,1)}) custom-call(s32[16]{0:T(128)S(4)} %get-tuple-element.5.map_ref, bf16[16,2,512,128]{3,2,1,0:T(8,128)(2,1)S(1)} %get-tuple-element.6.gat, bf16[2,1,4,4,128]{4,3,2,1,0:T(4,128)(2,1)S(1)} %get-tuple-element.7.part), custom_call_target="tpu_custom_call" | custom-call | tf_op jit(solution)/shard_map/pallas_call | solution.py:671

commit v6 on v5

--- a/solution.py
+++ b/solution.py
@@ -21,6 +21,7 @@
 SLOTS = 16
 PEERS = 16
 RANKS = 8
+STRIPE = 64
 HEADS = 64
 KVH = 8
 QROWS = STEPS * HEADS
@@ -572,16 +573,18 @@
         copy.wait_send()
 
 
-def place_kernel(map_ref, gat, part, out_hbm, part_out, sem, part_sem):
+def place_kernel(map_ref, gat, part, out_hbm, part_out, rows_buf, sem, part_sem):
     last = pltpu.make_async_copy(part, part_out, part_sem)
     last.start()
+    slots = [map_ref[group] for group in range(SLOTS)]
     copies = []
-    for group in range(SLOTS):
-        for layer in range(LAYERS):
+    for layer in range(LAYERS):
+        for n in range(ROWS // STRIPE):
+            rows = slice(n * STRIPE, (n + 1) * STRIPE)
+            for group in range(SLOTS):
+                rows_buf[layer, rows, group * HD : (group + 1) * HD] = gat[slots[group], layer, rows]
             copy = pltpu.make_async_copy(
-                gat.at[map_ref[group], layer],
-                out_hbm.at[layer, :, pl.ds(group * HD, HD)],
-                sem.at[group, layer],
+                rows_buf.at[layer, rows, :], out_hbm.at[layer, rows, :], sem.at[layer, n]
             )
             copy.start()
             copies.append(copy)
@@ -676,7 +679,11 @@
         ),
         in_specs=[smem, vmem, vmem],
         out_specs=(anywhere, anywhere),
-        scratch_shapes=[dma((SLOTS, LAYERS)), dma(())],
+        scratch_shapes=[
+            pltpu.VMEM((LAYERS, ROWS, SLOTS * HD), bf16),
+            dma((LAYERS, ROWS // STRIPE)),
+            dma(()),
+        ],
         compiler_params=pltpu.CompilerParams(vmem_limit_bytes=16 * MIB),
     )(chosen, gathered, part)
 

time: 35.4 us -> 35.3 us (level)
  no operation moved by 1% of the time
where the time goes in v6:
time: 35.3 us; the launch traced here: 35.2 us
  Pallas kernels  33.9 us (96%)
  between operations  1.29 us (4%)
    pallas_call x1, Pallas kernels, on_device(): pl.pallas_call(gather_kernel, out_shape=(pltpu.VMEM((SLOTS, LAYERS, ROWS,...  31.7 us
    pallas_call x1, Pallas kernels, on_device(): pl.pallas_call(place_kernel, out_shape=(jax.ShapeDtypeStruct((LAYERS, ROW...  2.21 us

profile of v6, /device:TPU:2, one launch (start us, length us, event | category | flops | bytes accessed | tf_op | source)
XLA Modules:
  0.0 35.2 jit_solution(5281280398087577589)
XLA Ops:
  1.3 31.7 %shard_map.122 = (bf16[16,2,512,128]{3,2,1,0:T(8,128)(2,1)S(1)}, bf16[2,1,4,4,128]{4,3,2,1,0:T(4,128)(2,1)S(1)}, s32[16]{0:T(128)S(4)}) custom-call(s32[16]{0:T(128)} %map_hbm.1, s32[1]{0:T(128)S(6)} %copy.13.len_ref, bf16[2,1,4,512]{3,2,1,0:T(4,128)(2,1)} %hid_hbm.1, bf16[2,512,2048]{2,1,0:T(8,128)(2,1)} %res_hbm.1, bf16[2,512,128]{2,1,0:T(8,128)(2,1)} %code_hbm.1, ...), custom_call_target="tpu_custom_call" | custom-call | tf_op jit(solution)/shard_map/pallas_call | solution.py:615
  33.0 2.2 %shard_map.123 = (bf16[2,512,2048]{2,1,0:T(8,128)(2,1)}, bf16[2,1,4,4,128]{4,3,2,1,0:T(4,128)(2,1)}) custom-call(s32[16]{0:T(128)S(4)} %get-tuple-element.5.map_ref, bf16[16,2,512,128]{3,2,1,0:T(8,128)(2,1)S(1)} %get-tuple-element.6.gat, bf16[2,1,4,4,128]{4,3,2,1,0:T(4,128)(2,1)S(1)} %get-tuple-element.7.part), custom_call_target="tpu_custom_call" | custom-call | tf_op jit(solution)/shard_map/pallas_call | solution.py:674
